TPU v7x, 1024 devices: a whole 4x4x32 slice. The times are simulated.
1024 devices in a mesh: depth: 4 (over y_hi, core), hx: 32 (over z), hy: 8 (over y_lo, x).
Axes of the slice: x: 4, y: 4 (y_hi: 2, y_lo: 2; y = y_hi * 2 + y_lo), z: 32, core: 2. Of those that a mesh axis runs over, the one named last changes fastest.
Arguments:
- fine_velocity: float32 [3, 16, 192, 3072], P(None, 'depth', 'hx', 'hy'), may hold values from -6 to 6
- fine_stress: float32 [6, 16, 192, 3072], P(None, 'depth', 'hx', 'hy'), may hold values from -3 to 3
- coarse_velocity: float32 [3, 8, 64, 1024], P(None, 'depth', 'hx', 'hy'), may hold values from -6 to 6
- coarse_stress: float32 [6, 8, 64, 1024], P(None, 'depth', 'hx', 'hy'), may hold values from -3 to 3
- iwan_states: float32 [10, 6, 16, 192, 3072], P(None, None, 'depth', 'hx', 'hy'), may hold values from -0.3 to 0.3
- fine_zones: int32 [16, 192, 3072], P('depth', 'hx', 'hy'), may hold values from 0 to 15
- coarse_zones: int32 [8, 64, 1024], P('depth', 'hx', 'hy'), may hold values from 0 to 15
- plastic: int32 [16, 192, 3072], P('depth', 'hx', 'hy'), may hold values from 0 to 1, as said below
- zone_buoyancy: float32 [16], replicated, may hold values from 0.5 to 1
- zone_lambda: float32 [16], replicated, may hold values from 0.1 to 0.3
- zone_mu: float32 [16], replicated, may hold values from 0.1 to 0.3
- iwan_share: float32 [10], replicated, may hold values from 0.3 to 3
- iwan_radius: float32 [10], replicated, may hold values from 0.01 to 0.3
Outputs:
- fine_velocity_out: float32 [3, 16, 192, 3072], P(None, 'depth', 'hx', 'hy')
- fine_stress_out: float32 [6, 16, 192, 3072], P(None, 'depth', 'hx', 'hy')
- coarse_velocity_out: float32 [3, 8, 64, 1024], P(None, 'depth', 'hx', 'hy')
- coarse_stress_out: float32 [6, 8, 64, 1024], P(None, 'depth', 'hx', 'hy')
Inputs may be any that keep to these rules, and one draw needn't show every extreme that they name: `plastic`: 1 marks a cell that follows the Iwan model, 0 an elastic cell.
All inputs are finite; a program needn't handle non-finite values.
Results may differ from a plain program's by a relative error of at most 0.0001.
Values sent between devices are 32-bit elements; how exact they have to be, the bound alone decides.
No kernel may reach another device: no remote copies, remote signals or barrier semaphores. Data moves between devices by JAX's collectives and lax.ppermute only.
A program may use at most 64 MiB of HBM per device.

v0:
```python
import functools

import jax
import jax.numpy as jnp
from jax import lax
from jax.experimental import pallas as pl
from jax.experimental.pallas import tpu as pltpu
from jax.sharding import PartitionSpec as P

DT = 0.4
NEAR = 9.0 / 8.0
FAR = 1.0 / 24.0
F32 = jnp.float32
ROWS, LANES = 6, 384
TILE = 128
STRESS = {"x": (0, 3, 4), "y": (1, 3, 5), "z": (2, 4, 5)}
SPEED = {"x": (0, 1, 2), "y": (0, 1, 2), "z": (0, 1, 2)}
MESSAGES = {"x": (4, 8, LANES), "y": (4, 8, TILE), "z": (6, 8, LANES)}


def roll(x, shift, axis):
    shift %= x.shape[axis]
    return x if shift == 0 else pltpu.roll(x, shift, axis)


def iota(shape, axis):
    return lax.broadcasted_iota(jnp.int32, shape, axis)


def stencil(get, forward, scale):
    near, far = NEAR * scale, FAR * scale
    if forward:
        return near * (get(1) - get(0)) - far * (get(2) - get(-1))
    return near * (get(0) - get(-1)) - far * (get(1) - get(-2))


def lookup(zones, table):
    total = jnp.zeros(zones.shape, F32)
    for member in range(table.shape[0]):
        total = jnp.where(zones == member, table[member], total)
    return total


class Fields:
    def __init__(self, fine, coarse, fine_room, coarse_room, sets, halos):
        self.fine_room, self.coarse_room, self.sets, self.halos = fine_room, coarse_room, sets, halos
        for c in range(fine.shape[0]):
            for z in range(4):
                fine_room[c, z, 0:ROWS] = fine[c, z]
                fine_room[c, z, ROWS:8] = jnp.zeros((2, LANES), F32)
            for z in range(2):
                coarse_room[c, z] = jnp.zeros((8, TILE), F32)
                coarse_room[c, z, 0:2] = coarse[c, 1 - z]

    def couple(self):
        bottom = (lax.axis_index("depth") == lax.axis_size("depth") - 1).astype(F32)
        comps = self.sets["z"]
        narrow, wide = iota((TILE, LANES), 0) * 3, iota((TILE, LANES), 1)
        repeat = jnp.where((wide >= narrow) & (wide < narrow + 3), 1.0, 0.0).astype(F32)
        narrow, wide = iota((LANES, TILE), 1) * 3, iota((LANES, TILE), 0)
        gather = jnp.where((wide >= narrow) & (wide < narrow + 3), bottom / 9.0, 0.0).astype(F32)
        dot = functools.partial(
            jnp.dot, precision=lax.Precision.HIGHEST, preferred_element_type=F32
        )
        row = iota((8, LANES), 0)
        self.below, self.above = {}, {}
        spread = dot(jnp.concatenate([self.coarse_room[c, 0] for c in comps], 0), repeat)
        means = dot(
            jnp.concatenate([self.fine_room[c, z] for c in comps for z in (3, 0)], 0), gather
        )
        for place, c in enumerate(comps):
            wide = spread[8 * place : 8 * place + 8]
            wide = jnp.where(row < 3, wide[0:1], wide[1:2])
            last = self.fine_room[c, 3]
            self.below[c, 4] = bottom * (2.0 / 3.0 * last + 1.0 / 3.0 * wide)
            self.below[c, 5] = bottom * (1.0 / 3.0 * last + 2.0 / 3.0 * wide)
            for step in range(2):
                at = 8 * (2 * place + step)
                part = means[at : at + 8]
                part = part + roll(part, -1, 0) + roll(part, -2, 0)
                self.above[c, -1 - step] = jnp.where(row[:, :TILE] == 0, part, roll(part, -2, 0))

    def fine_x(self, c, z):
        place = self.sets["x"].index(c)
        row = iota((8, LANES), 0)
        own = self.fine_room[c, z]
        before = jnp.where(row < ROWS, own, roll(self.halos["x"][0][place], 6 - 2 * z, 0))
        after = jnp.where(row < ROWS, own, roll(self.halos["x"][1][place], 6 - 2 * z, 0))
        return lambda off: own if off == 0 else roll(before if off < 0 else after, -off, 0)

    def fine_y(self, c, z):
        place = self.sets["y"].index(c)
        lane = iota((8, TILE), 1)
        before = roll(self.halos["y"][0][z], 2 * place, 1)
        after = roll(self.halos["y"][1][z], -2 * place, 1)
        whole = jnp.concatenate([self.fine_room[c, z], jnp.where(lane < 64, after, before)], 1)
        return lambda off: roll(whole, -off, 1)[:, :LANES]

    def fine_z(self, c, z):
        place = self.sets["z"].index(c)

        def get(off):
            at = z + off
            if at < 0:
                return self.halos["z"][0][2 * place + at + 2]
            if at < 4:
                return self.fine_room[c, at]
            return self.halos["z"][1][2 * place + at - 4] + self.below[c, at]

        return get

    def coarse_x(self, c, z):
        place = self.sets["x"].index(c)
        lanes = slice(place * TILE, place * TILE + TILE)
        row = iota((8, TILE), 0)
        before, after = self.halos["x"][0][3, :, lanes], self.halos["x"][1][3, :, lanes]
        own = self.coarse_room[c, z]
        whole = jnp.where(row < 4, roll(after, 2 - 2 * z, 0), roll(before, 6 - 2 * z, 0))
        whole = jnp.where(row < 2, own, whole)
        return lambda off: roll(whole, -off, 0)

    def coarse_y(self, c, z):
        place = self.sets["y"].index(c)
        lane = iota((8, TILE), 1)
        before = roll(roll(self.halos["y"][0][z], 2 * place, 1), 2, 0)
        after = roll(roll(self.halos["y"][1][z], -2 * place, 1), 2, 0)
        whole = jnp.concatenate([self.coarse_room[c, z], jnp.where(lane < 64, after, before)], 1)
        return lambda off: roll(whole, -off, 1)[:, :TILE]

    def coarse_z(self, c, z):
        place = self.sets["z"].index(c)
        lanes = slice(place * TILE, place * TILE + TILE)

        def get(off):
            at = z + off
            if at < 0:
                return roll(self.halos["z"][1][at + 2, :, lanes], 2, 0) + self.above[c, at]
            if at < 2:
                return self.coarse_room[c, at]
            return roll(self.halos["z"][0][at - 2, :, lanes], 2, 0)

        return get


def pack(fine, coarse, sets, out):
    for place, c in enumerate(sets["x"]):
        for z in range(4):
            slab = fine(c, z)
            out["x"][0][place, 2 * z : 2 * z + 2] = slab[0:2]
            out["x"][1][place, 2 * z : 2 * z + 2] = slab[4:6]
    for way in range(2):
        out["x"][way][3, 4:8] = jnp.zeros((4, LANES), F32)
        for place, c in enumerate(sets["x"]):
            for z in range(2):
                out["x"][way][3, 2 * z : 2 * z + 2, place * TILE : place * TILE + TILE] = coarse(c, z)
        for place, c in enumerate(sets["z"]):
            for layer in range(2):
                at = 2 * place + layer
                out["z"][way][at, 0:ROWS] = fine(c, layer + 2 * way)
                if place:
                    out["z"][way][at, ROWS:8] = jnp.zeros((2, LANES), F32)
                out["z"][way][layer, ROWS:8, place * TILE : place * TILE + TILE] = coarse(c, layer)
        for z in range(4):
            lane = iota((ROWS, TILE), 1)
            edge = slice(0, TILE) if way == 0 else slice(LANES - TILE, LANES)
            first, second, third = [fine(c, z)[:, edge] for c in sets["y"]]
            out["y"][way][z, 0:ROWS] = columns(first, second, third, lane, way)
            if z < 2:
                lane = iota((2, TILE), 1)
                first, second, third = [coarse(c, z) for c in sets["y"]]
                out["y"][way][z, ROWS:8] = columns(first, second, third, lane, way)
            else:
                out["y"][way][z, ROWS:8] = jnp.zeros((2, TILE), F32)


def columns(first, second, third, lane, way):
    if way == 0:
        return jnp.where(lane < 2, first, jnp.where(lane < 4, roll8(second, 2), roll8(third, 4)))
    return jnp.where(lane >= 126, first, jnp.where(lane >= 124, roll8(second, -2), roll8(third, -4)))


def roll8(x, shift):
    rows = x.shape[0]
    full = jnp.concatenate([x] * (8 // rows) + ([x[: 8 % rows]] if 8 % rows else []), 0)
    return roll(full, shift, 1)[:rows]


def both(refs):
    return {"x": refs[0:2], "y": refs[2:4], "z": refs[4:6]}


def first_kernel(fs, cs, *out):
    pack(lambda c, z: fs[c, z], lambda c, z: cs[c, 1 - z], STRESS, both(out))


def velocity_kernel(fv, cv, fs, cs, fzone, czone, table, *rest):
    halos, (nfv, ncv, *out), (fine_room, coarse_room) = rest[:6], rest[6:14], rest[14:]
    f = Fields(fs, cs, fine_room, coarse_room, STRESS, both(halos))
    f.couple()

    def forces(x, y, z, scale):
        def go(of, c, forward):
            return stencil(of(c), forward, scale)

        return (
            go(x, 0, True) + go(y, 3, False) + go(z, 4, False),
            go(x, 3, False) + go(y, 1, True) + go(z, 5, False),
            go(x, 4, False) + go(y, 5, False) + go(z, 2, True),
        )

    for at in range(4):
        gain = DT * lookup(fzone[at], table)
        found = forces(*[lambda c, of=of: of(c, at) for of in (f.fine_x, f.fine_y, f.fine_z)], 1.0)
        for c in range(3):
            nfv[c, at] = fv[c, at] + gain * found[c][0:ROWS]
    for at in range(2):
        gain = DT * lookup(czone[1 - at], table)
        found = forces(
            *[lambda c, of=of: of(c, at) for of in (f.coarse_x, f.coarse_y, f.coarse_z)], 1.0 / 3.0
        )
        for c in range(3):
            ncv[c, 1 - at] = cv[c, 1 - at] + gain * found[c][0:2]
    pack(lambda c, z: nfv[c, z], lambda c, z: ncv[c, 1 - z], SPEED, both(out))


def stress_kernel(
    last, fv, cv, fs, cs, fzone, czone, plastic, states, lame, shear, share, radius, *rest
):
    halos, rest = rest[:6], rest[6:]
    nfs, ncs = rest[:2]
    out, new_states = (None, None) if last else (rest[3:9], rest[2])
    fine_room, coarse_room = rest[-2:]
    f = Fields(fv, cv, fine_room, coarse_room, SPEED, both(halos))
    f.couple()
    whole = share[0]
    for k in range(1, share.shape[0]):
        whole = whole + share[k]
    per_share = 1.0 / jnp.full((8, TILE), whole, F32)
    per_share = jnp.concatenate([per_share] * 3, 1)[0:ROWS]

    def rates(x, y, z, scale):
        def go(of, c, forward):
            return stencil(of(c), forward, scale)

        return (
            go(x, 0, False),
            go(y, 1, False),
            go(z, 2, False),
            go(x, 1, True) + go(y, 0, True),
            go(x, 2, True) + go(z, 0, True),
            go(y, 2, True) + go(z, 1, True),
        )

    for at in range(4):
        e = rates(*[lambda c, of=of: of(c, at) for of in (f.fine_x, f.fine_y, f.fine_z)], 1.0)
        e = [part[0:ROWS] for part in e]
        zone = fzone[at]
        first, mu = lookup(zone, lame), lookup(zone, shear)
        twice = (2.0 * DT) * mu
        once = DT * mu
        dilation = e[0] + e[1] + e[2]
        third = dilation * (1.0 / 3.0)
        old = [fs[c, at] for c in range(6)]
        pressure = DT * first * dilation
        rise = [twice * e[c] for c in range(3)] + [once * e[c] for c in range(3, 6)]
        elastic = [old[c] + pressure + rise[c] for c in range(3)] + [old[c] + rise[c] for c in range(3, 6)]
        step = [twice * (e[c] - third) for c in range(3)] + rise[3:]
        step = [per_share * part for part in step]
        active = plastic[at] == 1
        sums = [jnp.zeros((ROWS, LANES), F32)] * 6
        for k in range(share.shape[0]):
            weight, limit = share[k], radius[k]
            before = [states[k, c, at] for c in range(6)]
            t = [before[c] + weight * step[c] for c in range(6)]
            size = 0.5 * (t[0] * t[0] + t[1] * t[1] + t[2] * t[2]) + (
                t[3] * t[3] + t[4] * t[4] + t[5] * t[5]
            )
            back = limit * lax.rsqrt(jnp.maximum(size, limit * limit))
            t = [part * back for part in t]
            sums = [a + b for a, b in zip(sums, t)]
            if not last:
                for c in range(6):
                    new_states[k, c, at] = jnp.where(active, t[c], before[c])
        mean = (old[0] + old[1] + old[2]) * (1.0 / 3.0) + (DT * first + twice * (1.0 / 3.0)) * dilation
        for c in range(6):
            nfs[c, at] = jnp.where(active, mean + sums[c] if c < 3 else sums[c], elastic[c])
    for at in range(2):
        e = rates(
            *[lambda c, of=of: of(c, at) for of in (f.coarse_x, f.coarse_y, f.coarse_z)], 1.0 / 3.0
        )
        e = [part[0:2] for part in e]
        zone = czone[1 - at]
        first, mu = lookup(zone, lame), lookup(zone, shear)
        pressure = DT * first * (e[0] + e[1] + e[2])
        for c in range(6):
            rise = (2.0 * DT if c < 3 else DT) * mu * e[c]
            ncs[c, 1 - at] = cs[c, 1 - at] + (pressure + rise if c < 3 else rise)
    if not last:
        pack(lambda c, z: nfs[c, z], lambda c, z: ncs[c, 1 - z], STRESS, both(out))


VMEM = pl.BlockSpec(memory_space=pltpu.VMEM)
SMEM = pl.BlockSpec(memory_space=pltpu.SMEM)
SENT = [jax.ShapeDtypeStruct(MESSAGES[d], F32) for d in "xyz" for _ in range(2)]


def call(body, operands, scalars, halos, outs, rooms, flops):
    shapes = [jax.ShapeDtypeStruct(s, F32) if isinstance(s, tuple) else s for s in outs]
    return pl.pallas_call(
        body,
        out_shape=shapes,
        in_specs=[VMEM] * len(operands) + [SMEM] * len(scalars) + [VMEM] * len(halos),
        out_specs=[VMEM] * len(shapes),
        scratch_shapes=[
            s for n in rooms for s in (pltpu.VMEM((n, 4, 8, LANES), F32), pltpu.VMEM((n, 2, 8, TILE), F32))
        ],
        compiler_params=pltpu.CompilerParams(vmem_limit_bytes=40 * 2**20),
        cost_estimate=pl.CostEstimate(flops=flops, bytes_accessed=flops, transcendentals=0),
    )(*operands, *scalars, *halos)


def exchange(sent):
    found = []
    for number, axis in enumerate(("hx", "hy", "depth")):
        back, on = sent[2 * number : 2 * number + 2]
        up = [(i, i + 1) for i in range(lax.axis_size(axis) - 1)]
        found.append(lax.ppermute(on, axis, up))
        found.append(lax.ppermute(back, axis, [(b, a) for a, b in up]))
    return found


def per_device(fv, fs, cv, cs, states, fzone, czone, plastic, buoyancy, lame, shear, share, radius):
    sent = call(first_kernel, [fs, cs], [], [], SENT, [], 10**5)
    for step in range(2):
        last = step == 1
        fv, cv, *sent = call(
            velocity_kernel,
            [fv, cv, fs, cs, fzone, czone],
            [buoyancy],
            exchange(sent),
            [fv.shape, cv.shape] + SENT,
            [6],
            10**6,
        )
        found = call(
            functools.partial(stress_kernel, last),
            [fv, cv, fs, cs, fzone, czone, plastic, states],
            [lame, shear, share, radius],
            exchange(sent),
            [fs.shape, cs.shape] + ([] if last else [states.shape] + SENT),
            [3],
            10**7,
        )
        if last:
            fs, cs = found
        else:
            fs, cs, states, *sent = found
    return fv, fs, cv, cs


def solution(mesh):
    field = P(None, "depth", "hx", "hy")
    ids = P("depth", "hx", "hy")
    return jax.shard_map(
        per_device,
        mesh=mesh,
        in_specs=(field,) * 4 + (P(None, None, "depth", "hx", "hy"),) + (ids,) * 3 + (P(),) * 5,
        out_specs=(field,) * 4,
        check_vma=False,
    )
```

profile of v0, /device:TPU:792, one launch (start us, length us, event | category | flops | bytes accessed | tf_op | source)
XLA Modules:
  0.0 124.4 jit_solution(16035372048100570162)
XLA Ops:
  2.5 1.9 %collective-permute-start.4 = (f32[6,8,384]{2,1,0:T(8,128)S(1)}, f32[6,8,384]{2,1,0:T(8,128)S(1)}, u32[]{:S(2)}, u32[]{:S(2)}) collective-permute-start(f32[6,8,384]{2,1,0:T(8,128)S(1)} %get-tuple-element.41), channel_id=1, source_target_pairs={{0,256},{256,512},{512,768},{1,257},{257,513},{513,769},{2,258},{2... | collective-permute-start | bytes 221192 | tf_op jit(solution)/shard_map/ppermute | solution.py:327
  4.4 5.1 %collective-permute-start.5 = (f32[6,8,384]{2,1,0:T(8,128)S(1)}, f32[6,8,384]{2,1,0:T(8,128)S(1)}, u32[]{:S(2)}, u32[]{:S(2)}) collective-permute-start(f32[6,8,384]{2,1,0:T(8,128)S(1)} %get-tuple-element.42), channel_id=1, source_target_pairs={{256,0},{512,256},{768,512},{257,1},{513,257},{769,513},{258,2},{5... | collective-permute-start | bytes 221192 | tf_op jit(solution)/shard_map/ppermute | solution.py:328
  9.5 2.9 %collective-permute-start = (f32[4,8,384]{2,1,0:T(8,128)S(1)}, f32[4,8,384]{2,1,0:T(8,128)S(1)}, u32[]{:S(2)}, u32[]{:S(2)}) collective-permute-start(f32[4,8,384]{2,1,0:T(8,128)S(1)} %get-tuple-element.37), channel_id=1, source_target_pairs={{0,8},{8,16},{16,24},{24,32},{32,40},{40,48},{48,56},{56,64},{64,7... | collective-permute-start | bytes 147464 | tf_op jit(solution)/shard_map/ppermute | solution.py:327
  12.5 4.1 %collective-permute-start.1 = (f32[4,8,384]{2,1,0:T(8,128)S(1)}, f32[4,8,384]{2,1,0:T(8,128)S(1)}, u32[]{:S(2)}, u32[]{:S(2)}) collective-permute-start(f32[4,8,384]{2,1,0:T(8,128)S(1)} %get-tuple-element.38), channel_id=1, source_target_pairs={{8,0},{16,8},{24,16},{32,24},{40,32},{48,40},{56,48},{64,56},{72,6... | collective-permute-start | bytes 147464 | tf_op jit(solution)/shard_map/ppermute | solution.py:328
  16.6 3.4 %collective-permute-start.2 = (f32[4,8,128]{2,1,0:T(8,128)S(1)}, f32[4,8,128]{2,1,0:T(8,128)S(1)}, u32[]{:S(2)}, u32[]{:S(2)}) collective-permute-start(f32[4,8,128]{2,1,0:T(8,128)S(1)} %get-tuple-element.39), channel_id=1, source_target_pairs={{0,1},{1,2},{2,3},{3,4},{4,5},{5,6},{6,7},{8,9},{9,10},{10,11},{11... | collective-permute-start | bytes 49160 | tf_op jit(solution)/shard_map/ppermute | solution.py:327
  20.0 4.3 %collective-permute-done.2.rest_2_ = f32[4,8,128]{2,1,0:T(8,128)S(1)} collective-permute-done((f32[4,8,128]{2,1,0:T(8,128)S(1)}, f32[4,8,128]{2,1,0:T(8,128)S(1)}, u32[]{:S(2)}, u32[]{:S(2)}) %collective-permute-start.2) | collective-permute-done | bytes 16416 | tf_op jit(solution)/shard_map/ppermute | solution.py:327
  24.4 2.7 %collective-permute-start.3 = (f32[4,8,128]{2,1,0:T(8,128)S(1)}, f32[4,8,128]{2,1,0:T(8,128)S(1)}, u32[]{:S(2)}, u32[]{:S(2)}) collective-permute-start(f32[4,8,128]{2,1,0:T(8,128)S(1)} %get-tuple-element.40), channel_id=1, source_target_pairs={{1,0},{2,1},{3,2},{4,3},{5,4},{6,5},{7,6},{9,8},{10,9},{11,10},{12... | collective-permute-start | bytes 49160 | tf_op jit(solution)/shard_map/ppermute | solution.py:328
  33.4 1.9 %collective-permute-start.10 = (f32[6,8,384]{2,1,0:T(8,128)S(1)}, f32[6,8,384]{2,1,0:T(8,128)S(1)}, u32[]{:S(2)}, u32[]{:S(2)}) collective-permute-start(f32[6,8,384]{2,1,0:T(8,128)S(1)} %get-tuple-element.49), channel_id=1, source_target_pairs={{0,256},{256,512},{512,768},{1,257},{257,513},{513,769},{2,258},{2... | collective-permute-start | bytes 221192 | tf_op jit(solution)/shard_map/ppermute | solution.py:327
  35.3 5.1 %collective-permute-start.11 = (f32[6,8,384]{2,1,0:T(8,128)S(1)}, f32[6,8,384]{2,1,0:T(8,128)S(1)}, u32[]{:S(2)}, u32[]{:S(2)}) collective-permute-start(f32[6,8,384]{2,1,0:T(8,128)S(1)} %get-tuple-element.50), channel_id=1, source_target_pairs={{256,0},{512,256},{768,512},{257,1},{513,257},{769,513},{258,2},{5... | collective-permute-start | bytes 221192 | tf_op jit(solution)/shard_map/ppermute | solution.py:328
  40.5 1.9 %collective-permute-start.6 = (f32[4,8,384]{2,1,0:T(8,128)S(1)}, f32[4,8,384]{2,1,0:T(8,128)S(1)}, u32[]{:S(2)}, u32[]{:S(2)}) collective-permute-start(f32[4,8,384]{2,1,0:T(8,128)S(1)} %get-tuple-element.45), channel_id=1, source_target_pairs={{0,8},{8,16},{16,24},{24,32},{32,40},{40,48},{48,56},{56,64},{64,7... | collective-permute-start | bytes 147464 | tf_op jit(solution)/shard_map/ppermute | solution.py:327
  42.4 5.1 %collective-permute-start.7 = (f32[4,8,384]{2,1,0:T(8,128)S(1)}, f32[4,8,384]{2,1,0:T(8,128)S(1)}, u32[]{:S(2)}, u32[]{:S(2)}) collective-permute-start(f32[4,8,384]{2,1,0:T(8,128)S(1)} %get-tuple-element.46), channel_id=1, source_target_pairs={{8,0},{16,8},{24,16},{32,24},{40,32},{48,40},{56,48},{64,56},{72,6... | collective-permute-start | bytes 147464 | tf_op jit(solution)/shard_map/ppermute | solution.py:328
  47.5 2.0 %collective-permute-start.8 = (f32[4,8,128]{2,1,0:T(8,128)S(1)}, f32[4,8,128]{2,1,0:T(8,128)S(1)}, u32[]{:S(2)}, u32[]{:S(2)}) collective-permute-start(f32[4,8,128]{2,1,0:T(8,128)S(1)} %get-tuple-element.47), channel_id=1, source_target_pairs={{0,1},{1,2},{2,3},{3,4},{4,5},{5,6},{6,7},{8,9},{9,10},{10,11},{11... | collective-permute-start | bytes 49160 | tf_op jit(solution)/shard_map/ppermute | solution.py:327
  49.6 5.7 %collective-permute-done.8.rest_2_ = f32[4,8,128]{2,1,0:T(8,128)S(1)} collective-permute-done((f32[4,8,128]{2,1,0:T(8,128)S(1)}, f32[4,8,128]{2,1,0:T(8,128)S(1)}, u32[]{:S(2)}, u32[]{:S(2)}) %collective-permute-start.8) | collective-permute-done | bytes 16416 | tf_op jit(solution)/shard_map/ppermute | solution.py:327
  55.3 2.7 %collective-permute-start.9 = (f32[4,8,128]{2,1,0:T(8,128)S(1)}, f32[4,8,128]{2,1,0:T(8,128)S(1)}, u32[]{:S(2)}, u32[]{:S(2)}) collective-permute-start(f32[4,8,128]{2,1,0:T(8,128)S(1)} %get-tuple-element.48), channel_id=1, source_target_pairs={{1,0},{2,1},{3,2},{4,3},{5,4},{6,5},{7,6},{9,8},{10,9},{11,10},{12... | collective-permute-start | bytes 49160 | tf_op jit(solution)/shard_map/ppermute | solution.py:328
  58.8 2.1 %copy.24.states = f32[10,6,4,6,384]{4,3,2,1,0:T(8,128)S(1)} copy(f32[10,6,4,6,384]{4,2,3,1,0:T(4,128)} %param.17) | data formatting | bytes 4423680 | tf_op args[4]
  61.0 2.3 %shard_map.158 = (f32[6,4,6,384]{3,2,1,0:T(8,128)S(1)}, f32[6,2,2,128]{3,2,1,0:T(2,128)S(1)}, f32[10,6,4,6,384]{4,3,2,1,0:T(8,128)S(1)}, f32[4,8,384]{2,1,0:T(8,...) custom-call(f32[3,4,6,384]{3,2,1,0:T(8,128)S(1)} %get-tuple-element., ...), custom_call_target="tpu_custom_call" | custom-call | flops 10000000 | bytes 10000000 | tf_op jit(solution)/shard_map/pallas_call | solution.py:309
  63.4 1.9 %collective-permute-start.16 = (f32[6,8,384]{2,1,0:T(8,128)S(1)}, f32[6,8,384]{2,1,0:T(8,128)S(1)}, u32[]{:S(2)}, u32[]{:S(2)}) collective-permute-start(f32[6,8,384]{2,1,0:T(8,128)S(1)} %get-tuple-element.57), channel_id=1, source_target_pairs={{0,256},{256,512},{512,768},{1,257},{257,513},{513,769},{2,258},{2... | collective-permute-start | bytes 221192 | tf_op jit(solution)/shard_map/ppermute | solution.py:327
  65.3 5.1 %collective-permute-start.17 = (f32[6,8,384]{2,1,0:T(8,128)S(1)}, f32[6,8,384]{2,1,0:T(8,128)S(1)}, u32[]{:S(2)}, u32[]{:S(2)}) collective-permute-start(f32[6,8,384]{2,1,0:T(8,128)S(1)} %get-tuple-element.58), channel_id=1, source_target_pairs={{256,0},{512,256},{768,512},{257,1},{513,257},{769,513},{258,2},{5... | collective-permute-start | bytes 221192 | tf_op jit(solution)/shard_map/ppermute | solution.py:328
  70.4 1.9 %collective-permute-start.12 = (f32[4,8,384]{2,1,0:T(8,128)S(1)}, f32[4,8,384]{2,1,0:T(8,128)S(1)}, u32[]{:S(2)}, u32[]{:S(2)}) collective-permute-start(f32[4,8,384]{2,1,0:T(8,128)S(1)} %get-tuple-element.53), channel_id=1, source_target_pairs={{0,8},{8,16},{16,24},{24,32},{32,40},{40,48},{48,56},{56,64},{64,7... | collective-permute-start | bytes 147464 | tf_op jit(solution)/shard_map/ppermute | solution.py:327
  72.4 5.1 %collective-permute-start.13 = (f32[4,8,384]{2,1,0:T(8,128)S(1)}, f32[4,8,384]{2,1,0:T(8,128)S(1)}, u32[]{:S(2)}, u32[]{:S(2)}) collective-permute-start(f32[4,8,384]{2,1,0:T(8,128)S(1)} %get-tuple-element.54), channel_id=1, source_target_pairs={{8,0},{16,8},{24,16},{32,24},{40,32},{48,40},{56,48},{64,56},{72,6... | collective-permute-start | bytes 147464 | tf_op jit(solution)/shard_map/ppermute | solution.py:328
  77.5 3.1 %collective-permute-start.14 = (f32[4,8,128]{2,1,0:T(8,128)S(1)}, f32[4,8,128]{2,1,0:T(8,128)S(1)}, u32[]{:S(2)}, u32[]{:S(2)}) collective-permute-start(f32[4,8,128]{2,1,0:T(8,128)S(1)} %get-tuple-element.55), channel_id=1, source_target_pairs={{0,1},{1,2},{2,3},{3,4},{4,5},{5,6},{6,7},{8,9},{9,10},{10,11},{11... | collective-permute-start | bytes 49160 | tf_op jit(solution)/shard_map/ppermute | solution.py:327
  80.6 4.6 %collective-permute-done.14.rest_2_ = f32[4,8,128]{2,1,0:T(8,128)S(1)} collective-permute-done((f32[4,8,128]{2,1,0:T(8,128)S(1)}, f32[4,8,128]{2,1,0:T(8,128)S(1)}, u32[]{:S(2)}, u32[]{:S(2)}) %collective-permute-start.14) | collective-permute-done | bytes 16416 | tf_op jit(solution)/shard_map/ppermute | solution.py:327
  85.3 2.7 %collective-permute-start.15 = (f32[4,8,128]{2,1,0:T(8,128)S(1)}, f32[4,8,128]{2,1,0:T(8,128)S(1)}, u32[]{:S(2)}, u32[]{:S(2)}) collective-permute-start(f32[4,8,128]{2,1,0:T(8,128)S(1)} %get-tuple-element.56), channel_id=1, source_target_pairs={{1,0},{2,1},{3,2},{4,3},{5,4},{6,5},{7,6},{9,8},{10,9},{11,10},{12... | collective-permute-start | bytes 49160 | tf_op jit(solution)/shard_map/ppermute | solution.py:328
  88.0 2.9 %collective-permute-done.15.rest_3_ = f32[4,8,128]{2,1,0:T(8,128)S(1)} collective-permute-done((f32[4,8,128]{2,1,0:T(8,128)S(1)}, f32[4,8,128]{2,1,0:T(8,128)S(1)}, u32[]{:S(2)}, u32[]{:S(2)}) %collective-permute-start.15) | collective-permute-done | bytes 16416 | tf_op jit(solution)/shard_map/ppermute | solution.py:328
  90.9 2.0 %shard_map.159 = (f32[3,4,6,384]{3,2,1,0:T(8,128)S(1)}, f32[3,2,2,128]{3,2,1,0:T(2,128)}, f32[4,8,384]{2,1,0:T(8,128)S(1)}, f32[4,8,384]{2,1,0:T(8,128)S(1)}, f3...) custom-call(f32[3,4,6,384]{3,2,1,0:T(8,128)S(1)} %get-tuple-element.43.f, ...), custom_call_target="tpu_custom_call" | custom-call | flops 1000000 | bytes 1000000 | tf_op jit(solution)/shard_map/pallas_call | solution.py:309
  94.8 5.1 %collective-permute-start.23 = (f32[6,8,384]{2,1,0:T(8,128)S(1)}, f32[6,8,384]{2,1,0:T(8,128)S(1)}, u32[]{:S(2)}, u32[]{:S(2)}) collective-permute-start(f32[6,8,384]{2,1,0:T(8,128)S(1)} %get-tuple-element.67), channel_id=1, source_target_pairs={{256,0},{512,256},{768,512},{257,1},{513,257},{769,513},{258,2},{5... | collective-permute-start | bytes 221192 | tf_op jit(solution)/shard_map/ppermute | solution.py:328
  101.9 5.1 %collective-permute-start.19 = (f32[4,8,384]{2,1,0:T(8,128)S(1)}, f32[4,8,384]{2,1,0:T(8,128)S(1)}, u32[]{:S(2)}, u32[]{:S(2)}) collective-permute-start(f32[4,8,384]{2,1,0:T(8,128)S(1)} %get-tuple-element.63), channel_id=1, source_target_pairs={{8,0},{16,8},{24,16},{32,24},{40,32},{48,40},{56,48},{64,56},{72,6... | collective-permute-start | bytes 147464 | tf_op jit(solution)/shard_map/ppermute | solution.py:328
  107.0 1.9 %collective-permute-start.20 = (f32[4,8,128]{2,1,0:T(8,128)S(1)}, f32[4,8,128]{2,1,0:T(8,128)S(1)}, u32[]{:S(2)}, u32[]{:S(2)}) collective-permute-start(f32[4,8,128]{2,1,0:T(8,128)S(1)} %get-tuple-element.64), channel_id=1, source_target_pairs={{0,1},{1,2},{2,3},{3,4},{4,5},{5,6},{6,7},{8,9},{9,10},{10,11},{11... | collective-permute-start | bytes 49160 | tf_op jit(solution)/shard_map/ppermute | solution.py:327
  108.9 5.8 %collective-permute-done.20.rest_2_ = f32[4,8,128]{2,1,0:T(8,128)S(1)} collective-permute-done((f32[4,8,128]{2,1,0:T(8,128)S(1)}, f32[4,8,128]{2,1,0:T(8,128)S(1)}, u32[]{:S(2)}, u32[]{:S(2)}) %collective-permute-start.20) | collective-permute-done | bytes 16416 | tf_op jit(solution)/shard_map/ppermute | solution.py:327
  114.8 2.7 %collective-permute-start.21 = (f32[4,8,128]{2,1,0:T(8,128)S(1)}, f32[4,8,128]{2,1,0:T(8,128)S(1)}, u32[]{:S(2)}, u32[]{:S(2)}) collective-permute-start(f32[4,8,128]{2,1,0:T(8,128)S(1)} %get-tuple-element.65), channel_id=1, source_target_pairs={{1,0},{2,1},{3,2},{4,3},{5,4},{6,5},{7,6},{9,8},{10,9},{11,10},{12... | collective-permute-start | bytes 49160 | tf_op jit(solution)/shard_map/ppermute | solution.py:328
  118.1 2.2 %collective-permute-done.21.rest_3_ = f32[4,8,128]{2,1,0:T(8,128)S(1)} collective-permute-done((f32[4,8,128]{2,1,0:T(8,128)S(1)}, f32[4,8,128]{2,1,0:T(8,128)S(1)}, u32[]{:S(2)}, u32[]{:S(2)}) %collective-permute-start.21) | collective-permute-done | bytes 16416 | tf_op jit(solution)/shard_map/ppermute | solution.py:328
  121.1 2.5 %shard_map.160 = (f32[6,4,6,384]{3,2,1,0:T(8,128)S(1)}, f32[6,2,2,128]{3,2,1,0:T(2,128)}) custom-call(f32[3,4,6,384]{3,2,1,0:T(8,128)S(1)} %get-tuple-element.70.fv, f32[3,2,2,128]{3,2,1,0:T(2,128)S(1)} %copy-done.5, f32[6,4,6,384]{3,2,1,0:T(8,128)S(1)} %get-tuple-element.51.fs, f32[6,2,2,128]{3,2,1,0:T(2,128)S(1)} %get-tuple-element.52.cs, ...), custom_call_target="tpu_custom_call" | custom-call | flops 10000000 | bytes 10000000 | tf_op jit(solution)/shard_map/pallas_call | solution.py:309
  (52 shorter events, 14.8 us)
Async XLA Ops:
  1.6 0.7 copy-start
  2.5 27.5 %collective-permute-start.4 = (f32[6,8,384]{2,1,0:T(8,128)S(1)}, f32[6,8,384]{2,1,0:T(8,128)S(1)}, u32[]{:S(2)}, u32[]{:S(2)}) collective-permute-start(f32[6,8,384]{2,1,0:T(8,128)S(1)} %get-tuple-element.41), channel_id=1, source_target_pairs={{0,256},{256,512},{512,768},{1,257},{257,513},{513,769},{2,258},{2... | collective-permute-start | bytes 221192 | tf_op jit(solution)/shard_map/ppermute | solution.py:327
  4.4 25.6 %collective-permute-start.5 = (f32[6,8,384]{2,1,0:T(8,128)S(1)}, f32[6,8,384]{2,1,0:T(8,128)S(1)}, u32[]{:S(2)}, u32[]{:S(2)}) collective-permute-start(f32[6,8,384]{2,1,0:T(8,128)S(1)} %get-tuple-element.42), channel_id=1, source_target_pairs={{256,0},{512,256},{768,512},{257,1},{513,257},{769,513},{258,2},{5... | collective-permute-start | bytes 221192 | tf_op jit(solution)/shard_map/ppermute | solution.py:328
  9.5 20.4 %collective-permute-start = (f32[4,8,384]{2,1,0:T(8,128)S(1)}, f32[4,8,384]{2,1,0:T(8,128)S(1)}, u32[]{:S(2)}, u32[]{:S(2)}) collective-permute-start(f32[4,8,384]{2,1,0:T(8,128)S(1)} %get-tuple-element.37), channel_id=1, source_target_pairs={{0,8},{8,16},{16,24},{24,32},{32,40},{40,48},{48,56},{56,64},{64,7... | collective-permute-start | bytes 147464 | tf_op jit(solution)/shard_map/ppermute | solution.py:327
  12.5 17.5 %collective-permute-start.1 = (f32[4,8,384]{2,1,0:T(8,128)S(1)}, f32[4,8,384]{2,1,0:T(8,128)S(1)}, u32[]{:S(2)}, u32[]{:S(2)}) collective-permute-start(f32[4,8,384]{2,1,0:T(8,128)S(1)} %get-tuple-element.38), channel_id=1, source_target_pairs={{8,0},{16,8},{24,16},{32,24},{40,32},{48,40},{56,48},{64,56},{72,6... | collective-permute-start | bytes 147464 | tf_op jit(solution)/shard_map/ppermute | solution.py:328
  16.6 7.7 %collective-permute-start.2 = (f32[4,8,128]{2,1,0:T(8,128)S(1)}, f32[4,8,128]{2,1,0:T(8,128)S(1)}, u32[]{:S(2)}, u32[]{:S(2)}) collective-permute-start(f32[4,8,128]{2,1,0:T(8,128)S(1)} %get-tuple-element.39), channel_id=1, source_target_pairs={{0,1},{1,2},{2,3},{3,4},{4,5},{5,6},{6,7},{8,9},{9,10},{10,11},{11... | collective-permute-start | bytes 49160 | tf_op jit(solution)/shard_map/ppermute | solution.py:327
  24.4 5.6 %collective-permute-start.3 = (f32[4,8,128]{2,1,0:T(8,128)S(1)}, f32[4,8,128]{2,1,0:T(8,128)S(1)}, u32[]{:S(2)}, u32[]{:S(2)}) collective-permute-start(f32[4,8,128]{2,1,0:T(8,128)S(1)} %get-tuple-element.40), channel_id=1, source_target_pairs={{1,0},{2,1},{3,2},{4,3},{5,4},{6,5},{7,6},{9,8},{10,9},{11,10},{12... | collective-permute-start | bytes 49160 | tf_op jit(solution)/shard_map/ppermute | solution.py:328
  27.9 33.1 %copy-start.3 = (s32[2,2,128]{2,1,0:T(2,128)S(1)}, s32[2,2,128]{2,1,0:T(2,128)}, u32[]{:S(2)}) copy-start(s32[2,2,128]{2,1,0:T(2,128)} %czone.7) | copy-start | bytes 6148
  27.9 33.1 %copy-start.6 = (f32[16]{0:T(128)S(1)}, f32[16]{0:T(128)}, u32[]{:S(2)}) copy-start(f32[16]{0:T(128)} %lame.3) | copy-start | bytes 196
  27.9 33.1 %copy-start.7 = (f32[16]{0:T(128)S(1)}, f32[16]{0:T(128)}, u32[]{:S(2)}) copy-start(f32[16]{0:T(128)} %shear.3) | copy-start | bytes 196
  27.9 33.1 %copy-start.8 = (f32[10]{0:T(128)S(1)}, f32[10]{0:T(128)}, u32[]{:S(2)}) copy-start(f32[10]{0:T(128)} %share.3) | copy-start | bytes 124
  27.9 33.1 %copy-start.9 = (f32[10]{0:T(128)S(1)}, f32[10]{0:T(128)}, u32[]{:S(2)}) copy-start(f32[10]{0:T(128)} %radius.3) | copy-start | bytes 124
  28.9 32.2 %copy-start.1 = (f32[6,2,2,128]{3,2,1,0:T(2,128)S(1)}, f32[6,2,2,128]{3,2,1,0:T(2,128)}, u32[]{:S(2)}) copy-start(f32[6,2,2,128]{3,2,1,0:T(2,128)} %cs.5) | copy-start | bytes 36868
  33.4 27.6 %collective-permute-start.10 = (f32[6,8,384]{2,1,0:T(8,128)S(1)}, f32[6,8,384]{2,1,0:T(8,128)S(1)}, u32[]{:S(2)}, u32[]{:S(2)}) collective-permute-start(f32[6,8,384]{2,1,0:T(8,128)S(1)} %get-tuple-element.49), channel_id=1, source_target_pairs={{0,256},{256,512},{512,768},{1,257},{257,513},{513,769},{2,258},{2... | collective-permute-start | bytes 221192 | tf_op jit(solution)/shard_map/ppermute | solution.py:327
  35.3 25.6 %collective-permute-start.11 = (f32[6,8,384]{2,1,0:T(8,128)S(1)}, f32[6,8,384]{2,1,0:T(8,128)S(1)}, u32[]{:S(2)}, u32[]{:S(2)}) collective-permute-start(f32[6,8,384]{2,1,0:T(8,128)S(1)} %get-tuple-element.50), channel_id=1, source_target_pairs={{256,0},{512,256},{768,512},{257,1},{513,257},{769,513},{258,2},{5... | collective-permute-start | bytes 221192 | tf_op jit(solution)/shard_map/ppermute | solution.py:328
  40.5 20.4 %collective-permute-start.6 = (f32[4,8,384]{2,1,0:T(8,128)S(1)}, f32[4,8,384]{2,1,0:T(8,128)S(1)}, u32[]{:S(2)}, u32[]{:S(2)}) collective-permute-start(f32[4,8,384]{2,1,0:T(8,128)S(1)} %get-tuple-element.45), channel_id=1, source_target_pairs={{0,8},{8,16},{16,24},{24,32},{32,40},{40,48},{48,56},{56,64},{64,7... | collective-permute-start | bytes 147464 | tf_op jit(solution)/shard_map/ppermute | solution.py:327
  42.4 18.5 %collective-permute-start.7 = (f32[4,8,384]{2,1,0:T(8,128)S(1)}, f32[4,8,384]{2,1,0:T(8,128)S(1)}, u32[]{:S(2)}, u32[]{:S(2)}) collective-permute-start(f32[4,8,384]{2,1,0:T(8,128)S(1)} %get-tuple-element.46), channel_id=1, source_target_pairs={{8,0},{16,8},{24,16},{32,24},{40,32},{48,40},{56,48},{64,56},{72,6... | collective-permute-start | bytes 147464 | tf_op jit(solution)/shard_map/ppermute | solution.py:328
  47.5 7.7 %collective-permute-start.8 = (f32[4,8,128]{2,1,0:T(8,128)S(1)}, f32[4,8,128]{2,1,0:T(8,128)S(1)}, u32[]{:S(2)}, u32[]{:S(2)}) collective-permute-start(f32[4,8,128]{2,1,0:T(8,128)S(1)} %get-tuple-element.47), channel_id=1, source_target_pairs={{0,1},{1,2},{2,3},{3,4},{4,5},{5,6},{6,7},{8,9},{9,10},{10,11},{11... | collective-permute-start | bytes 49160 | tf_op jit(solution)/shard_map/ppermute | solution.py:327
  55.3 5.6 %collective-permute-start.9 = (f32[4,8,128]{2,1,0:T(8,128)S(1)}, f32[4,8,128]{2,1,0:T(8,128)S(1)}, u32[]{:S(2)}, u32[]{:S(2)}) collective-permute-start(f32[4,8,128]{2,1,0:T(8,128)S(1)} %get-tuple-element.48), channel_id=1, source_target_pairs={{1,0},{2,1},{3,2},{4,3},{5,4},{6,5},{7,6},{9,8},{10,9},{11,10},{12... | collective-permute-start | bytes 49160 | tf_op jit(solution)/shard_map/ppermute | solution.py:328
  60.9 30.0 %copy-start.11 = (f32[16]{0:T(128)S(1)}, f32[16]{0:T(128)}, u32[]{:S(2)}) copy-start(f32[16]{0:T(128)} %table.3) | copy-start | bytes 196
  63.4 27.5 %collective-permute-start.16 = (f32[6,8,384]{2,1,0:T(8,128)S(1)}, f32[6,8,384]{2,1,0:T(8,128)S(1)}, u32[]{:S(2)}, u32[]{:S(2)}) collective-permute-start(f32[6,8,384]{2,1,0:T(8,128)S(1)} %get-tuple-element.57), channel_id=1, source_target_pairs={{0,256},{256,512},{512,768},{1,257},{257,513},{513,769},{2,258},{2... | collective-permute-start | bytes 221192 | tf_op jit(solution)/shard_map/ppermute | solution.py:327
  65.3 25.6 %collective-permute-start.17 = (f32[6,8,384]{2,1,0:T(8,128)S(1)}, f32[6,8,384]{2,1,0:T(8,128)S(1)}, u32[]{:S(2)}, u32[]{:S(2)}) collective-permute-start(f32[6,8,384]{2,1,0:T(8,128)S(1)} %get-tuple-element.58), channel_id=1, source_target_pairs={{256,0},{512,256},{768,512},{257,1},{513,257},{769,513},{258,2},{5... | collective-permute-start | bytes 221192 | tf_op jit(solution)/shard_map/ppermute | solution.py:328
  70.4 20.4 %collective-permute-start.12 = (f32[4,8,384]{2,1,0:T(8,128)S(1)}, f32[4,8,384]{2,1,0:T(8,128)S(1)}, u32[]{:S(2)}, u32[]{:S(2)}) collective-permute-start(f32[4,8,384]{2,1,0:T(8,128)S(1)} %get-tuple-element.53), channel_id=1, source_target_pairs={{0,8},{8,16},{16,24},{24,32},{32,40},{40,48},{48,56},{56,64},{64,7... | collective-permute-start | bytes 147464 | tf_op jit(solution)/shard_map/ppermute | solution.py:327
  72.4 18.5 %collective-permute-start.13 = (f32[4,8,384]{2,1,0:T(8,128)S(1)}, f32[4,8,384]{2,1,0:T(8,128)S(1)}, u32[]{:S(2)}, u32[]{:S(2)}) collective-permute-start(f32[4,8,384]{2,1,0:T(8,128)S(1)} %get-tuple-element.54), channel_id=1, source_target_pairs={{8,0},{16,8},{24,16},{32,24},{40,32},{48,40},{56,48},{64,56},{72,6... | collective-permute-start | bytes 147464 | tf_op jit(solution)/shard_map/ppermute | solution.py:328
  77.5 7.7 %collective-permute-start.14 = (f32[4,8,128]{2,1,0:T(8,128)S(1)}, f32[4,8,128]{2,1,0:T(8,128)S(1)}, u32[]{:S(2)}, u32[]{:S(2)}) collective-permute-start(f32[4,8,128]{2,1,0:T(8,128)S(1)} %get-tuple-element.55), channel_id=1, source_target_pairs={{0,1},{1,2},{2,3},{3,4},{4,5},{5,6},{6,7},{8,9},{9,10},{10,11},{11... | collective-permute-start | bytes 49160 | tf_op jit(solution)/shard_map/ppermute | solution.py:327
  85.3 5.6 %collective-permute-start.15 = (f32[4,8,128]{2,1,0:T(8,128)S(1)}, f32[4,8,128]{2,1,0:T(8,128)S(1)}, u32[]{:S(2)}, u32[]{:S(2)}) collective-permute-start(f32[4,8,128]{2,1,0:T(8,128)S(1)} %get-tuple-element.56), channel_id=1, source_target_pairs={{1,0},{2,1},{3,2},{4,3},{5,4},{6,5},{7,6},{9,8},{10,9},{11,10},{12... | collective-permute-start | bytes 49160 | tf_op jit(solution)/shard_map/ppermute | solution.py:328
  92.9 27.5 %collective-permute-start.22 = (f32[6,8,384]{2,1,0:T(8,128)S(1)}, f32[6,8,384]{2,1,0:T(8,128)S(1)}, u32[]{:S(2)}, u32[]{:S(2)}) collective-permute-start(f32[6,8,384]{2,1,0:T(8,128)S(1)} %get-tuple-element.66), channel_id=1, source_target_pairs={{0,256},{256,512},{512,768},{1,257},{257,513},{513,769},{2,258},{2... | collective-permute-start | bytes 221192 | tf_op jit(solution)/shard_map/ppermute | solution.py:327
  94.8 25.6 %collective-permute-start.23 = (f32[6,8,384]{2,1,0:T(8,128)S(1)}, f32[6,8,384]{2,1,0:T(8,128)S(1)}, u32[]{:S(2)}, u32[]{:S(2)}) collective-permute-start(f32[6,8,384]{2,1,0:T(8,128)S(1)} %get-tuple-element.67), channel_id=1, source_target_pairs={{256,0},{512,256},{768,512},{257,1},{513,257},{769,513},{258,2},{5... | collective-permute-start | bytes 221192 | tf_op jit(solution)/shard_map/ppermute | solution.py:328
  99.9 20.4 %collective-permute-start.18 = (f32[4,8,384]{2,1,0:T(8,128)S(1)}, f32[4,8,384]{2,1,0:T(8,128)S(1)}, u32[]{:S(2)}, u32[]{:S(2)}) collective-permute-start(f32[4,8,384]{2,1,0:T(8,128)S(1)} %get-tuple-element.62), channel_id=1, source_target_pairs={{0,8},{8,16},{16,24},{24,32},{32,40},{40,48},{48,56},{56,64},{64,7... | collective-permute-start | bytes 147464 | tf_op jit(solution)/shard_map/ppermute | solution.py:327
  101.9 18.5 %collective-permute-start.19 = (f32[4,8,384]{2,1,0:T(8,128)S(1)}, f32[4,8,384]{2,1,0:T(8,128)S(1)}, u32[]{:S(2)}, u32[]{:S(2)}) collective-permute-start(f32[4,8,384]{2,1,0:T(8,128)S(1)} %get-tuple-element.63), channel_id=1, source_target_pairs={{8,0},{16,8},{24,16},{32,24},{40,32},{48,40},{56,48},{64,56},{72,6... | collective-permute-start | bytes 147464 | tf_op jit(solution)/shard_map/ppermute | solution.py:328
  107.0 7.7 %collective-permute-start.20 = (f32[4,8,128]{2,1,0:T(8,128)S(1)}, f32[4,8,128]{2,1,0:T(8,128)S(1)}, u32[]{:S(2)}, u32[]{:S(2)}) collective-permute-start(f32[4,8,128]{2,1,0:T(8,128)S(1)} %get-tuple-element.64), channel_id=1, source_target_pairs={{0,1},{1,2},{2,3},{3,4},{4,5},{5,6},{6,7},{8,9},{9,10},{10,11},{11... | collective-permute-start | bytes 49160 | tf_op jit(solution)/shard_map/ppermute | solution.py:327
  114.8 5.6 %collective-permute-start.21 = (f32[4,8,128]{2,1,0:T(8,128)S(1)}, f32[4,8,128]{2,1,0:T(8,128)S(1)}, u32[]{:S(2)}, u32[]{:S(2)}) collective-permute-start(f32[4,8,128]{2,1,0:T(8,128)S(1)} %get-tuple-element.65), channel_id=1, source_target_pairs={{1,0},{2,1},{3,2},{4,3},{5,4},{6,5},{7,6},{9,8},{10,9},{11,10},{12... | collective-permute-start | bytes 49160 | tf_op jit(solution)/shard_map/ppermute | solution.py:328
  (4 other events, 2.7 us)
where the time goes:
time: 125 us; the launch traced here: 124 us
  starting transfers between devices  77.8 us (62%)
  waiting for transfers between devices  26.8 us (21%)
  local copies, waits for them, and re-layouts  10.4 us (8%)
  Pallas kernels  8.31 us (7%)
    ppermute x12, starting transfers between devices, exchange(): found.append(lax.ppermute(back, axis, [(b, a) for a, b in up]))  50.9 us
    ppermute x12, starting transfers between devices, exchange(): found.append(lax.ppermute(on, axis, up))  26.8 us
    ppermute x12, waiting for transfers between devices, exchange(): found.append(lax.ppermute(on, axis, up))  20.5 us
    unnamed x31, local copies, waits for them, and re-layouts  10.4 us
    pallas_call x5, Pallas kernels, call(): pl.pallas_call(body, out_shape=shapes, in_specs=[VMEM] * len(operands) +...  8.31 us
    ppermute x12, waiting for transfers between devices, exchange(): found.append(lax.ppermute(back, axis, [(b, a) for a, b in up]))  6.29 us
  transfers between devices with their start and end apart: 24, of which 7 were waited for; matrix products, arithmetic and copies ran while one was open for 4% of the time, Pallas kernels for 0%

commit v1 on v0

v1 whole, which is shorter than its diff:
```python
import functools

import jax
import jax.numpy as jnp
from jax import lax
from jax.experimental import pallas as pl
from jax.experimental.pallas import tpu as pltpu
from jax.sharding import PartitionSpec as P

DT = 0.4
NEAR = 9.0 / 8.0
FAR = 1.0 / 24.0
F32 = jnp.float32
NX, NZ, OWN, TILE = 6, 4, 384, 128
WIDE = OWN + TILE
CWIDE = 2 * TILE
STRESS = {"x": (0, 3, 4), "y": (1, 3, 5), "z": (2, 4, 5)}
SPEED = {"x": (0, 1, 2), "y": (0, 1, 2), "z": (0, 1, 2)}
FINE_TILES = (
    [(18, [("s", c) for c in range(3)]), (18, [("s", c) for c in range(3, 6)])]
    + [(12, [("v", 0), ("v", 1), ("v", 2), ("zone", None), ("plastic", None)])]
    + [(6, [("q", (n // 6, n % 6)) for n in range(10 * t, 10 * t + 10)]) for t in range(6)]
)
COARSE_TILES = [
    (8, [("s", c) for c in range(6)]),
    (8, [("v", 0), ("v", 1), ("v", 2), ("zone", None)]),
]
N_FINE = len(FINE_TILES)
Y_MESSAGE = (N_FINE * NX + len(COARSE_TILES), 4, TILE)
X_MESSAGE = (8, 4, WIDE)
Z_MESSAGE = (11, 4, WIDE)


def roll(x, shift, axis):
    shift %= x.shape[axis]
    return x if shift == 0 else pltpu.roll(x, shift, axis)


def iota(shape, axis):
    return lax.broadcasted_iota(jnp.int32, shape, axis)


def stencil(get, forward, scale):
    near, far = NEAR * scale, FAR * scale
    if forward:
        return near * (get(1) - get(0)) - far * (get(2) - get(-1))
    return near * (get(0) - get(-1)) - far * (get(1) - get(-2))


def lookup(zones, table):
    total = jnp.zeros(zones.shape, F32)
    for member in range(table.shape[0]):
        total = jnp.where(zones == float(member + 1), table[member], total)
    return total


def pack_y(get, width, names, rows, way):
    lane = iota((rows, TILE), 1)
    tile = jnp.zeros((rows, TILE), F32)
    for slot, name in enumerate(names):
        start = 2 * width * slot + (width if way == 0 else 0)
        edge = roll(get(name), 2 * width * slot + width, 1)
        tile = jnp.where((lane >= start) & (lane < start + width), edge, tile)
    return tile


def merged(before, after, width):
    lane = iota(before.shape, 1)
    return jnp.where(lane % (2 * width) < width, before, after)


def halo_of(tile, width, slot):
    return roll(tile, -(2 * width * slot + width), 1)


def pack_kernel(fs, fv, zone, plastic, states, cs, cv, czone, back, on):
    for way, out in ((0, back), (1, on)):
        lanes = slice(0, TILE) if way == 0 else slice(OWN - TILE, OWN)

        def fine(name, x):
            kind, c = name
            if kind == "s":
                return fs[c, x, :, lanes]
            if kind == "v":
                return fv[c, x, :, lanes]
            if kind == "q":
                return states[c[0], c[1], x, :, lanes]
            if kind == "zone":
                return zone[x, :, lanes].astype(F32) + 1.0
            return plastic[x, :, lanes].astype(F32)

        def pair(name, x):
            return jnp.concatenate([fine(name, x), fine(name, x + 1)], 0)

        for t, (width, names) in enumerate(FINE_TILES):
            for x in range(0, NX, 2):
                tile = pack_y(functools.partial(pair, x=x), width, names, 8, way)
                out[t * NX + x] = tile[0:4]
                out[t * NX + x + 1] = tile[4:8]

        def coarse(name):
            kind, c = name
            if kind == "zone":
                rows = [czone[1 - z].astype(F32) + 1.0 for z in range(2)]
            else:
                rows = [(cs if kind == "s" else cv)[c, 1 - z] for z in range(2)]
            return jnp.concatenate(rows * 2, 0)

        for t, (width, names) in enumerate(COARSE_TILES):
            out[N_FINE * NX + t] = pack_y(coarse, width, names, 8, way)[0:4]


def start_kernel(fs, fv, zone, plastic, cs, cv, czone, before, after, *rest):
    nfs, nfv, nzone, nplastic, ncs, ncv, nczone = rest[:7]
    for x in range(NX):
        for c in range(6):
            nfs[c, x, :, 0:OWN] = fs[c, x]
        for c in range(3):
            nfv[c, x, :, 0:OWN] = fv[c, x]
        nzone[x, :, 0:OWN] = zone[x].astype(F32) + 1.0
        nplastic[x, :, 0:OWN] = plastic[x].astype(F32)
    fine = {"s": nfs, "v": nfv, "zone": nzone, "plastic": nplastic}
    for t, (width, names) in enumerate(FINE_TILES[:3]):
        for x in range(0, NX, 2):
            at = t * NX + x
            two = [jnp.concatenate([m[at], m[at + 1]], 0) for m in (before, after)]
            tile = merged(two[0], two[1], width)
            for slot, (kind, c) in enumerate(names):
                halo = halo_of(tile, width, slot)
                for i in range(2):
                    to = (x + i,) if c is None else (c, x + i)
                    fine[kind][to + (slice(None), slice(OWN, WIDE))] = halo[4 * i : 4 * i + 4]
    for z in range(2):
        for c in range(6):
            ncs[c, z, :, 0:TILE] = cs[c, 1 - z]
        for c in range(3):
            ncv[c, z, :, 0:TILE] = cv[c, 1 - z]
        nczone[z, :, 0:TILE] = czone[1 - z].astype(F32) + 1.0
    coarse = {"s": ncs, "v": ncv, "zone": nczone}
    for t, (width, names) in enumerate(COARSE_TILES):
        two = [jnp.concatenate([m[N_FINE * NX + t]] * 2, 0) for m in (before, after)]
        tile = merged(two[0], two[1], width)
        for slot, (kind, c) in enumerate(names):
            halo = halo_of(tile, width, slot)
            for z in range(2):
                to = (z,) if c is None else (c, z)
                coarse[kind][to + (slice(None), slice(TILE, CWIDE))] = halo[2 * z : 2 * z + 2]
    pack(nfs, ncs, STRESS, rest[7:])


def pack(fine, coarse, sets, out):
    for way in range(2):
        to_x, to_z = out[way], out[2 + way]
        for place, c in enumerate(sets["x"]):
            for i in range(2):
                to_x[2 * place + i] = fine[c, 4 * way + i]
        for place, c in enumerate(sets["z"]):
            for x in range(NX):
                rows = slice(2 * (x % 2), 2 * (x % 2) + 2)
                to_z[3 * place + x // 2, rows] = fine[c, x, 2 * way : 2 * way + 2]
        for out_ref, first, comps in ((to_x, 6, sets["x"]), (to_z, 9, sets["z"])):
            for place, c in enumerate(comps):
                for z in range(2):
                    out_ref[first + place // 2, 2 * z : 2 * z + 2, coarse_lanes(place)] = coarse[c, z]
            out_ref[first + 1, :, CWIDE:WIDE] = jnp.zeros((4, CWIDE), F32)


def coarse_lanes(place):
    return slice(CWIDE * (place % 2), CWIDE * (place % 2) + CWIDE)


class Fields:
    def __init__(self, fine, coarse, sets, halos, rooms):
        self.fine, self.coarse, self.sets = fine, coarse, sets
        self.x_before, self.x_after, self.z_before, self.z_after = halos
        self.z_room, self.c_room, self.narrow_room, self.wide_room = rooms
        self.couple()
        for place, c in enumerate(sets["z"]):
            for x in range(NX):
                at, rows = 3 * place + x // 2, slice(2 * (x % 2), 2 * (x % 2) + 2)
                self.z_room[place, x, 0:4] = fine[c, x]
                self.z_room[place, x, 4:6] = self.z_after[at, rows] + self.below[c, x]
                self.z_room[place, x, 6:8] = self.z_before[at, rows]
        for c in range(coarse.shape[0]):
            for z in range(2):
                self.c_room[c, z, 0:2] = coarse[c, z]
                if c in sets["x"]:
                    place = sets["x"].index(c)
                    spot = (6 + place // 2, slice(2 * z, 2 * z + 2), coarse_lanes(place))
                    self.c_room[c, z, 2:4] = self.x_after[spot]
                    self.c_room[c, z, 6:8] = self.x_before[spot]
                else:
                    self.c_room[c, z, 2:8] = jnp.zeros((6, CWIDE), F32)

    def couple(self):
        bottom = (lax.axis_index("depth") == lax.axis_size("depth") - 1).astype(F32)
        comps = self.sets["z"]

        def match(shape, wide_axis):
            wide, narrow = iota(shape, wide_axis), iota(shape, 1 - wide_axis)
            first = jnp.where(narrow < CWIDE - TILE // 2, narrow, narrow - CWIDE) * 3
            wide = jnp.where(wide < WIDE - TILE // 2, wide, wide - WIDE)
            return (wide >= first) & (wide < first + 3)

        repeat = jnp.where(match((CWIDE, WIDE), 1), 1.0, 0.0).astype(F32)
        gather = jnp.where(match((WIDE, CWIDE), 0), bottom / 9.0, 0.0).astype(F32)
        dot = functools.partial(
            jnp.dot, precision=lax.Precision.HIGHEST, preferred_element_type=F32
        )
        narrow, wide = self.narrow_room, self.wide_room
        narrow[6:8] = jnp.zeros((2, CWIDE), F32)
        wide[12:16] = jnp.zeros((4, WIDE), F32)
        for place, c in enumerate(comps):
            narrow[2 * place : 2 * place + 2] = self.coarse[c, 0]
            for step, z in enumerate((3, 0)):
                for r in range(2):
                    at = 4 * place + 2 * step + r
                    line = [self.fine[c, 3 * r + i, z : z + 1] for i in range(3)]
                    wide[at : at + 1] = line[0] + line[1] + line[2]
        spread = dot(narrow[...], repeat)
        means = dot(wide[...], gather)
        self.below, self.above = {}, {}
        far = iota((2, WIDE), 0) == 1
        for place, c in enumerate(comps):
            for x in range(NX):
                last, line = self.fine[c, x, 3:4], spread[2 * place + x // 3 : 2 * place + x // 3 + 1]
                near, deep = 2.0 / 3.0 * last + 1.0 / 3.0 * line, 1.0 / 3.0 * last + 2.0 / 3.0 * line
                self.below[c, x] = bottom * jnp.where(far, deep, near)
            for step in range(2):
                at = 4 * place + 2 * step
                self.above[c, -1 - step] = means[at : at + 2]

    def fine_x(self, c, x):
        place = self.sets["x"].index(c)

        def get(off):
            at = x + off
            if at < 0:
                return self.x_before[2 * place + at + 2]
            if at >= NX:
                return self.x_after[2 * place + at - NX]
            return self.fine[c, at]

        return get

    def fine_y(self, c, x):
        first = x - x % 2
        both = jnp.concatenate([self.fine[c, first], self.fine[c, first + 1]], 0)
        rows = slice(4 * (x % 2), 4 * (x % 2) + 4)
        return lambda off: roll(both, -off, 1)[rows]

    def fine_z(self, c, x):
        whole = self.z_room[self.sets["z"].index(c), x]
        return lambda off: roll(whole, -off, 0)[0:4]

    def coarse_x(self, c, z):
        whole = self.c_room[c, z]
        return lambda off: roll(whole, -off, 0)[0:2]

    def coarse_y(self, c, z):
        whole = self.c_room[c, z]
        return lambda off: roll(whole, -off, 1)[0:2]

    def coarse_z(self, c, z):
        place = self.sets["z"].index(c)

        def piece(message, at):
            return message[9 + place // 2, 2 * at : 2 * at + 2, coarse_lanes(place)]

        def get(off):
            at = z + off
            if at < 0:
                return piece(self.z_after, at + 2) + self.above[c, at]
            if at < 2:
                return self.coarse[c, at]
            return piece(self.z_before, at - 2)

        return get

    def fine_ways(self, x):
        return [lambda c, of=of: of(c, x) for of in (self.fine_x, self.fine_y, self.fine_z)]

    def coarse_ways(self, z):
        return [lambda c, of=of: of(c, z) for of in (self.coarse_x, self.coarse_y, self.coarse_z)]


def forces(x, y, z, scale):
    def go(of, c, forward):
        return stencil(of(c), forward, scale)

    return (
        go(x, 0, True) + go(y, 3, False) + go(z, 4, False),
        go(x, 3, False) + go(y, 1, True) + go(z, 5, False),
        go(x, 4, False) + go(y, 5, False) + go(z, 2, True),
    )


def rates(x, y, z, scale):
    def go(of, c, forward):
        return stencil(of(c), forward, scale)

    return (
        go(x, 0, False),
        go(y, 1, False),
        go(z, 2, False),
        go(x, 1, True) + go(y, 0, True),
        go(x, 2, True) + go(z, 0, True),
        go(y, 2, True) + go(z, 1, True),
    )


def velocity_kernel(last, fv, cv, fs, cs, zone, czone, table, *rest):
    halos, rest = rest[:4], rest[4:]
    nfv, ncv, *out = rest[:6]
    f = Fields(fs, cs, STRESS, halos, rest[-4:])
    for x in range(NX):
        gain = DT * lookup(zone[x], table)
        found = forces(*f.fine_ways(x), 1.0)
        for c in range(3):
            new = fv[c, x] + gain * found[c]
            nfv[c, x] = new
            if last:
                rest[6][c, x] = new[:, 0:OWN]
    for z in range(2):
        gain = DT * lookup(czone[z], table)
        found = forces(*f.coarse_ways(z), 1.0 / 3.0)
        for c in range(3):
            new = cv[c, z] + gain * found[c]
            ncv[c, z] = new
            if last:
                rest[7][c, 1 - z] = new[:, 0:TILE]
    pack(nfv, ncv, SPEED, out)


def stress_kernel(last, fv, cv, fs, cs, zone, czone, plastic, states, *rest):
    before, after = (None, None) if last else rest[:2]
    rest = rest if last else rest[2:]
    lame, shear, share, radius = rest[:4]
    halos, rest = rest[4:8], rest[8:]
    nfs, ncs = rest[:2]
    f = Fields(fv, cv, SPEED, halos, rest[-4:])
    width = OWN if last else WIDE
    total = share[0]
    for k in range(1, share.shape[0]):
        total = total + share[k]
    per_share = 1.0 / jnp.full((4, TILE), total, F32)
    per_share = jnp.concatenate([per_share] * (width // TILE), 1)
    tiles = {}

    def state(k, c, x):
        own = states[k, c, x]
        if last:
            return own
        tile, slot = divmod(6 * k + c, 10)
        at = (3 + tile) * NX + x
        if (tile, x) not in tiles:
            first = at - x % 2
            two = [jnp.concatenate([m[first], m[first + 1]], 0) for m in (before, after)]
            tiles[tile, x] = merged(two[0], two[1], 6)
        halo = halo_of(tiles[tile, x], 6, slot)
        return jnp.concatenate([own, halo[4 * (x % 2) : 4 * (x % 2) + 4]], 1)

    for x in range(NX):
        e = [part[:, 0:width] for part in rates(*f.fine_ways(x), 1.0)]
        ids = zone[x, :, 0:width]
        first, mu = lookup(ids, lame), lookup(ids, shear)
        twice = (2.0 * DT) * mu
        once = DT * mu
        dilation = e[0] + e[1] + e[2]
        third = dilation * (1.0 / 3.0)
        old = [fs[c, x, :, 0:width] for c in range(6)]
        pressure = DT * first * dilation
        rise = [twice * e[c] for c in range(3)] + [once * e[c] for c in range(3, 6)]
        elastic = [old[c] + pressure + rise[c] for c in range(3)] + [old[c] + rise[c] for c in range(3, 6)]
        step = [twice * (e[c] - third) for c in range(3)] + rise[3:]
        step = [per_share * part for part in step]
        active = plastic[x, :, 0:width] == 1.0
        sums = [jnp.zeros((4, width), F32)] * 6
        for k in range(share.shape[0]):
            weight, limit = share[k], radius[k]
            was = [state(k, c, x) for c in range(6)]
            t = [was[c] + weight * step[c] for c in range(6)]
            size = 0.5 * (t[0] * t[0] + t[1] * t[1] + t[2] * t[2]) + (
                t[3] * t[3] + t[4] * t[4] + t[5] * t[5]
            )
            scale = limit * lax.rsqrt(jnp.maximum(size, limit * limit))
            t = [part * scale for part in t]
            sums = [a + b for a, b in zip(sums, t)]
            if not last:
                for c in range(6):
                    rest[2][k, c, x] = jnp.where(active, t[c], was[c])[:, 0:OWN]
        mean = (old[0] + old[1] + old[2]) * (1.0 / 3.0) + (DT * first + twice * (1.0 / 3.0)) * dilation
        for c in range(6):
            nfs[c, x] = jnp.where(active, mean + sums[c] if c < 3 else sums[c], elastic[c])
    for z in range(2):
        e = rates(*f.coarse_ways(z), 1.0 / 3.0)
        first, mu = lookup(czone[z], lame), lookup(czone[z], shear)
        pressure = DT * first * (e[0] + e[1] + e[2])
        for c in range(6):
            rise = (2.0 * DT if c < 3 else DT) * mu * e[c]
            new = cs[c, z] + (pressure + rise if c < 3 else rise)
            if last:
                ncs[c, 1 - z] = new[:, 0:TILE]
            else:
                ncs[c, z] = new
    if not last:
        pack(nfs, ncs, STRESS, rest[3:7])


VMEM = pl.BlockSpec(memory_space=pltpu.VMEM)
SMEM = pl.BlockSpec(memory_space=pltpu.SMEM)
SENT = [X_MESSAGE, X_MESSAGE, Z_MESSAGE, Z_MESSAGE]


def call(body, operands, scalars, halos, outs, fields, flops):
    rooms = [(3, NX, 8, WIDE), (fields, 2, 8, CWIDE), (8, CWIDE), (16, WIDE)] if fields else []
    return pl.pallas_call(
        body,
        out_shape=[jax.ShapeDtypeStruct(s, F32) for s in outs],
        in_specs=[VMEM] * len(operands) + [SMEM] * len(scalars) + [VMEM] * len(halos),
        out_specs=[VMEM] * len(outs),
        scratch_shapes=[pltpu.VMEM(s, F32) for s in rooms],
        compiler_params=pltpu.CompilerParams(vmem_limit_bytes=40 * 2**20),
        cost_estimate=pl.CostEstimate(flops=flops, bytes_accessed=flops, transcendentals=0),
    )(*operands, *scalars, *halos)


def exchange(axes, sent):
    found = []
    for number, axis in enumerate(axes):
        back, on = sent[2 * number : 2 * number + 2]
        up = [(i, i + 1) for i in range(lax.axis_size(axis) - 1)]
        found.append(lax.ppermute(on, axis, up))
        found.append(lax.ppermute(back, axis, [(b, a) for a, b in up]))
    return found


def per_device(fv, fs, cv, cs, states, zone, czone, plastic, buoyancy, lame, shear, share, radius):
    fv, fs, states, zone, plastic = [jnp.swapaxes(a, -3, -2) for a in (fv, fs, states, zone, plastic)]
    sent = call(pack_kernel, [fs, fv, zone, plastic, states, cs, cv, czone], [], [], [Y_MESSAGE] * 2, 0, 10**6)
    y_halo = exchange(["hy"], sent)
    grown = [(6, NX, 4, WIDE), (3, NX, 4, WIDE), (NX, 4, WIDE), (NX, 4, WIDE)]
    grown += [(6, 2, 2, CWIDE), (3, 2, 2, CWIDE), (2, 2, CWIDE)]
    fs, fv, zone, plastic, cs, cv, czone, *sent = call(
        start_kernel, [fs, fv, zone, plastic, cs, cv, czone], [], y_halo, grown + SENT, 0, 10**6
    )
    for step in range(2):
        last = step == 1
        outs = [fv.shape, cv.shape] + SENT + ([(3, NX, 4, OWN), (3, 2, 2, TILE)] if last else [])
        found = call(
            functools.partial(velocity_kernel, last),
            [fv, cv, fs, cs, zone, czone],
            [buoyancy],
            exchange(["hx", "depth"], sent),
            outs,
            6,
            10**6,
        )
        fv, cv, *sent = found[:6]
        if last:
            fv_out, cv_out = found[6:]
            outs = [(6, NX, 4, OWN), (6, 2, 2, TILE)]
        else:
            outs = [fs.shape, cs.shape, states.shape] + SENT
        found = call(
            functools.partial(stress_kernel, last),
            [fv, cv, fs, cs, zone, czone, plastic, states] + ([] if last else y_halo),
            [lame, shear, share, radius],
            exchange(["hx", "depth"], sent),
            outs,
            3,
            10**7,
        )
        if last:
            fs, cs = found
        else:
            fs, cs, states, *sent = found
    return jnp.swapaxes(fv_out, 1, 2), jnp.swapaxes(fs, 1, 2), cv_out, cs


def solution(mesh):
    field = P(None, "depth", "hx", "hy")
    ids = P("depth", "hx", "hy")
    return jax.shard_map(
        per_device,
        mesh=mesh,
        in_specs=(field,) * 4 + (P(None, None, "depth", "hx", "hy"),) + (ids,) * 3 + (P(),) * 5,
        out_specs=(field,) * 4,
        check_vma=False,
    )
```

time: 125 us -> 106 us (0.85)
  the two profiles are of different devices: /device:TPU:792 before, /device:TPU:374 now
where the time goes in v1:
time: 106 us; the launch traced here: 105 us
  starting transfers between devices  58.7 us (55%)
  waiting for transfers between devices  26.2 us (25%)
  Pallas kernels  11.8 us (11%)
  local copies, waits for them, and re-layouts  7.12 us (7%)
    ppermute x9, starting transfers between devices, exchange(): found.append(lax.ppermute(back, axis, [(b, a) for a, b in up]))  32.6 us
    ppermute x9, starting transfers between devices, exchange(): found.append(lax.ppermute(on, axis, up))  26.1 us
    ppermute x9, waiting for transfers between devices, exchange(): found.append(lax.ppermute(back, axis, [(b, a) for a, b in up]))  24.4 us
    pallas_call x6, Pallas kernels, call(): pl.pallas_call(body, out_shape=[jax.ShapeDtypeStruct(s, F32) for s in out...  11.8 us
    unnamed x34, local copies, waits for them, and re-layouts  7.12 us
  transfers between devices with their start and end apart: 18, of which 9 were waited for; matrix products, arithmetic and copies ran while one was open for 0% of the time, Pallas kernels for 0%

profile of v1, /device:TPU:374, one launch (start us, length us, event | category | flops | bytes accessed | tf_op | source)
XLA Modules:
  0.0 104.8 jit_solution(13650842617255710766)
XLA Ops:
  0.7 1.6 %copy-done = f32[10,6,4,6,384]{4,2,3,1,0:T(4,128)S(1)} copy-done((f32[10,6,4,6,384]{4,2,3,1,0:T(4,128)S(1)}, f32[10,6,4,6,384]{4,2,3,1,0:T(4,128)}, u32[]{:S(2)}) %copy-start) | copy-done | bytes 2211864
  2.3 0.9 copy-done.2
  3.3 0.9 copy-done.3
  4.2 0.8 copy-done.4
  8.3 3.2 %collective-permute-start = (f32[56,4,128]{2,1,0:T(4,128)S(1)}, f32[56,4,128]{2,1,0:T(4,128)S(1)}, u32[]{:S(2)}, u32[]{:S(2)}) collective-permute-start(f32[56,4,128]{2,1,0:T(4,128)S(1)} %get-tuple-element.40), channel_id=1, source_target_pairs={{0,1},{1,2},{2,3},{3,4},{4,5},{5,6},{6,7},{8,9},{9,10},{10,11},{11... | collective-permute-start | bytes 344072 | tf_op jit(solution)/shard_map/ppermute | solution.py:433
  11.6 2.7 %collective-permute-start.1 = (f32[56,4,128]{2,1,0:T(4,128)S(1)}, f32[56,4,128]{2,1,0:T(4,128)S(1)}, u32[]{:S(2)}, u32[]{:S(2)}) collective-permute-start(f32[56,4,128]{2,1,0:T(4,128)S(1)} %get-tuple-element.41), channel_id=1, source_target_pairs={{1,0},{2,1},{3,2},{4,3},{5,4},{6,5},{7,6},{9,8},{10,9},{11,10},{12... | collective-permute-start | bytes 344072 | tf_op jit(solution)/shard_map/ppermute | solution.py:434
  14.3 0.9 collective-permute-done.before.rest_0_
  15.3 5.1 %collective-permute-done.1.after.rest_1_ = f32[56,4,128]{2,1,0:T(4,128)S(1)} collective-permute-done((f32[56,4,128]{2,1,0:T(4,128)S(1)}, f32[56,4,128]{2,1,0:T(4,128)S(1)}, u32[]{:S(2)}, u32[]{:S(2)}) %collective-permute-start.1) | collective-permute-done | bytes 114720 | tf_op jit(solution)/shard_map/ppermute | solution.py:434
  20.5 1.9 %collective-permute-start.4 = (f32[11,4,512]{2,1,0:T(4,128)S(1)}, f32[11,4,512]{2,1,0:T(4,128)S(1)}, u32[]{:S(2)}, u32[]{:S(2)}) collective-permute-start(f32[11,4,512]{2,1,0:T(4,128)S(1)} %get-tuple-element.50), channel_id=1, source_target_pairs={{0,256},{256,512},{512,768},{1,257},{257,513},{513,769},{2,258},{2... | collective-permute-start | bytes 270344 | tf_op jit(solution)/shard_map/ppermute | solution.py:433
  22.5 5.1 %collective-permute-start.5 = (f32[11,4,512]{2,1,0:T(4,128)S(1)}, f32[11,4,512]{2,1,0:T(4,128)S(1)}, u32[]{:S(2)}, u32[]{:S(2)}) collective-permute-start(f32[11,4,512]{2,1,0:T(4,128)S(1)} %get-tuple-element.51), channel_id=1, source_target_pairs={{256,0},{512,256},{768,512},{257,1},{513,257},{769,513},{258,2},{5... | collective-permute-start | bytes 270344 | tf_op jit(solution)/shard_map/ppermute | solution.py:434
  27.6 5.0 %collective-permute-start.2 = (f32[8,4,512]{2,1,0:T(4,128)S(1)}, f32[8,4,512]{2,1,0:T(4,128)S(1)}, u32[]{:S(2)}, u32[]{:S(2)}) collective-permute-start(f32[8,4,512]{2,1,0:T(4,128)S(1)} %get-tuple-element.48), channel_id=1, source_target_pairs={{0,8},{8,16},{16,24},{24,32},{32,40},{40,48},{48,56},{56,64},{64,7... | collective-permute-start | bytes 196616 | tf_op jit(solution)/shard_map/ppermute | solution.py:433
  32.7 1.9 %collective-permute-start.3 = (f32[8,4,512]{2,1,0:T(4,128)S(1)}, f32[8,4,512]{2,1,0:T(4,128)S(1)}, u32[]{:S(2)}, u32[]{:S(2)}) collective-permute-start(f32[8,4,512]{2,1,0:T(4,128)S(1)} %get-tuple-element.49), channel_id=1, source_target_pairs={{8,0},{16,8},{24,16},{32,24},{40,32},{48,40},{56,48},{64,56},{72,6... | collective-permute-start | bytes 196616 | tf_op jit(solution)/shard_map/ppermute | solution.py:434
  34.6 5.4 %collective-permute-done.3.rest_1_ = f32[8,4,512]{2,1,0:T(4,128)S(1)} collective-permute-done((f32[8,4,512]{2,1,0:T(4,128)S(1)}, f32[8,4,512]{2,1,0:T(4,128)S(1)}, u32[]{:S(2)}, u32[]{:S(2)}) %collective-permute-start.3) | collective-permute-done | bytes 65568 | tf_op jit(solution)/shard_map/ppermute | solution.py:434
  40.1 1.7 %shard_map.158 = (f32[3,6,4,512]{3,2,1,0:T(4,128)S(1)}, f32[3,2,2,256]{3,2,1,0:T(2,128)S(1)}, f32[8,4,512]{2,1,0:T(4,128)S(1)}, f32[8,4,512]{2,1,0:T(4,128)S(1)}...) custom-call(f32[3,6,4,512]{3,2,1,0:T(4,128)S(1)} %get-tuple-element.42.fv, ...), custom_call_target="tpu_custom_call" | custom-call | flops 1000000 | bytes 1000000 | tf_op jit(solution)/shard_map/pallas_call | solution.py:417
  41.8 1.9 %collective-permute-start.8 = (f32[11,4,512]{2,1,0:T(4,128)S(1)}, f32[11,4,512]{2,1,0:T(4,128)S(1)}, u32[]{:S(2)}, u32[]{:S(2)}) collective-permute-start(f32[11,4,512]{2,1,0:T(4,128)S(1)} %get-tuple-element.57), channel_id=1, source_target_pairs={{0,256},{256,512},{512,768},{1,257},{257,513},{513,769},{2,258},{2... | collective-permute-start | bytes 270344 | tf_op jit(solution)/shard_map/ppermute | solution.py:433
  43.7 5.1 %collective-permute-start.9 = (f32[11,4,512]{2,1,0:T(4,128)S(1)}, f32[11,4,512]{2,1,0:T(4,128)S(1)}, u32[]{:S(2)}, u32[]{:S(2)}) collective-permute-start(f32[11,4,512]{2,1,0:T(4,128)S(1)} %get-tuple-element.58), channel_id=1, source_target_pairs={{256,0},{512,256},{768,512},{257,1},{513,257},{769,513},{258,2},{5... | collective-permute-start | bytes 270344 | tf_op jit(solution)/shard_map/ppermute | solution.py:434
  48.9 2.6 %collective-permute-start.6 = (f32[8,4,512]{2,1,0:T(4,128)S(1)}, f32[8,4,512]{2,1,0:T(4,128)S(1)}, u32[]{:S(2)}, u32[]{:S(2)}) collective-permute-start(f32[8,4,512]{2,1,0:T(4,128)S(1)} %get-tuple-element.55), channel_id=1, source_target_pairs={{0,8},{8,16},{16,24},{24,32},{32,40},{40,48},{48,56},{56,64},{64,7... | collective-permute-start | bytes 196616 | tf_op jit(solution)/shard_map/ppermute | solution.py:433
  51.5 3.2 %collective-permute-start.7 = (f32[8,4,512]{2,1,0:T(4,128)S(1)}, f32[8,4,512]{2,1,0:T(4,128)S(1)}, u32[]{:S(2)}, u32[]{:S(2)}) collective-permute-start(f32[8,4,512]{2,1,0:T(4,128)S(1)} %get-tuple-element.56), channel_id=1, source_target_pairs={{8,0},{16,8},{24,16},{32,24},{40,32},{48,40},{56,48},{64,56},{72,6... | collective-permute-start | bytes 196616 | tf_op jit(solution)/shard_map/ppermute | solution.py:434
  55.0 3.8 %collective-permute-done.7.rest_7_ = f32[8,4,512]{2,1,0:T(4,128)S(1)} collective-permute-done((f32[8,4,512]{2,1,0:T(4,128)S(1)}, f32[8,4,512]{2,1,0:T(4,128)S(1)}, u32[]{:S(2)}, u32[]{:S(2)}) %collective-permute-start.7) | collective-permute-done | bytes 65568 | tf_op jit(solution)/shard_map/ppermute | solution.py:434
  58.9 3.8 %shard_map.159 = (f32[6,6,4,512]{3,2,1,0:T(4,128)S(1)}, f32[6,2,2,256]{3,2,1,0:T(2,128)S(1)}, f32[10,6,6,4,384]{4,3,2,1,0:T(4,128)S(1)}, f32[8,4,512]{2,1,0:T(4,...) custom-call(f32[3,6,4,512]{3,2,1,0:T(4,128)S(1)} %get-tuple-element.52.fv, ...), custom_call_target="tpu_custom_call" | custom-call | flops 10000000 | bytes 10000000 | tf_op jit(solution)/shard_map/pallas_call | solution.py:417
  62.7 1.9 %collective-permute-start.12 = (f32[11,4,512]{2,1,0:T(4,128)S(1)}, f32[11,4,512]{2,1,0:T(4,128)S(1)}, u32[]{:S(2)}, u32[]{:S(2)}) collective-permute-start(f32[11,4,512]{2,1,0:T(4,128)S(1)} %get-tuple-element.63), channel_id=1, source_target_pairs={{0,256},{256,512},{512,768},{1,257},{257,513},{513,769},{2,258},{2... | collective-permute-start | bytes 270344 | tf_op jit(solution)/shard_map/ppermute | solution.py:433
  64.7 5.1 %collective-permute-start.13 = (f32[11,4,512]{2,1,0:T(4,128)S(1)}, f32[11,4,512]{2,1,0:T(4,128)S(1)}, u32[]{:S(2)}, u32[]{:S(2)}) collective-permute-start(f32[11,4,512]{2,1,0:T(4,128)S(1)} %get-tuple-element.64), channel_id=1, source_target_pairs={{256,0},{512,256},{768,512},{257,1},{513,257},{769,513},{258,2},{5... | collective-permute-start | bytes 270344 | tf_op jit(solution)/shard_map/ppermute | solution.py:434
  69.8 3.6 %collective-permute-start.10 = (f32[8,4,512]{2,1,0:T(4,128)S(1)}, f32[8,4,512]{2,1,0:T(4,128)S(1)}, u32[]{:S(2)}, u32[]{:S(2)}) collective-permute-start(f32[8,4,512]{2,1,0:T(4,128)S(1)} %get-tuple-element.61), channel_id=1, source_target_pairs={{0,8},{8,16},{16,24},{24,32},{32,40},{40,48},{48,56},{56,64},{64,7... | collective-permute-start | bytes 196616 | tf_op jit(solution)/shard_map/ppermute | solution.py:433
  73.5 2.2 %collective-permute-start.11 = (f32[8,4,512]{2,1,0:T(4,128)S(1)}, f32[8,4,512]{2,1,0:T(4,128)S(1)}, u32[]{:S(2)}, u32[]{:S(2)}) collective-permute-start(f32[8,4,512]{2,1,0:T(4,128)S(1)} %get-tuple-element.62), channel_id=1, source_target_pairs={{8,0},{16,8},{24,16},{32,24},{40,32},{48,40},{56,48},{64,56},{72,6... | collective-permute-start | bytes 196616 | tf_op jit(solution)/shard_map/ppermute | solution.py:434
  76.0 4.9 %collective-permute-done.11.rest_1_ = f32[8,4,512]{2,1,0:T(4,128)S(1)} collective-permute-done((f32[8,4,512]{2,1,0:T(4,128)S(1)}, f32[8,4,512]{2,1,0:T(4,128)S(1)}, u32[]{:S(2)}, u32[]{:S(2)}) %collective-permute-start.11) | collective-permute-done | bytes 65568 | tf_op jit(solution)/shard_map/ppermute | solution.py:434
  80.8 2.3 %shard_map.160 = (f32[3,6,4,512]{3,2,1,0:T(4,128)S(1)}, f32[3,2,2,256]{3,2,1,0:T(2,128)S(1)}, f32[8,4,512]{2,1,0:T(4,128)S(1)}, f32[8,4,512]{2,1,0:T(4,128)S(1)}...) custom-call(f32[3,6,4,512]{3,2,1,0:T(4,128)S(1)} %get-tuple-element., ...), custom_call_target="tpu_custom_call" | custom-call | flops 1000000 | bytes 1000000 | tf_op jit(solution)/shard_map/pallas_call | solution.py:417
  83.2 1.9 %collective-permute-start.16 = (f32[11,4,512]{2,1,0:T(4,128)S(1)}, f32[11,4,512]{2,1,0:T(4,128)S(1)}, u32[]{:S(2)}, u32[]{:S(2)}) collective-permute-start(f32[11,4,512]{2,1,0:T(4,128)S(1)} %get-tuple-element.71), channel_id=1, source_target_pairs={{0,256},{256,512},{512,768},{1,257},{257,513},{513,769},{2,258},{2... | collective-permute-start | bytes 270344 | tf_op jit(solution)/shard_map/ppermute | solution.py:433
  85.1 5.1 %collective-permute-start.17 = (f32[11,4,512]{2,1,0:T(4,128)S(1)}, f32[11,4,512]{2,1,0:T(4,128)S(1)}, u32[]{:S(2)}, u32[]{:S(2)}) collective-permute-start(f32[11,4,512]{2,1,0:T(4,128)S(1)} %get-tuple-element.72), channel_id=1, source_target_pairs={{256,0},{512,256},{768,512},{257,1},{513,257},{769,513},{258,2},{5... | collective-permute-start | bytes 270344 | tf_op jit(solution)/shard_map/ppermute | solution.py:434
  90.3 3.9 %collective-permute-start.14 = (f32[8,4,512]{2,1,0:T(4,128)S(1)}, f32[8,4,512]{2,1,0:T(4,128)S(1)}, u32[]{:S(2)}, u32[]{:S(2)}) collective-permute-start(f32[8,4,512]{2,1,0:T(4,128)S(1)} %get-tuple-element.69), channel_id=1, source_target_pairs={{0,8},{8,16},{16,24},{24,32},{32,40},{40,48},{48,56},{56,64},{64,7... | collective-permute-start | bytes 196616 | tf_op jit(solution)/shard_map/ppermute | solution.py:433
  94.2 1.9 %collective-permute-start.15 = (f32[8,4,512]{2,1,0:T(4,128)S(1)}, f32[8,4,512]{2,1,0:T(4,128)S(1)}, u32[]{:S(2)}, u32[]{:S(2)}) collective-permute-start(f32[8,4,512]{2,1,0:T(4,128)S(1)} %get-tuple-element.70), channel_id=1, source_target_pairs={{8,0},{16,8},{24,16},{32,24},{40,32},{48,40},{56,48},{64,56},{72,6... | collective-permute-start | bytes 196616 | tf_op jit(solution)/shard_map/ppermute | solution.py:434
  96.4 5.1 %collective-permute-done.15.rest_5_ = f32[8,4,512]{2,1,0:T(4,128)S(1)} collective-permute-done((f32[8,4,512]{2,1,0:T(4,128)S(1)}, f32[8,4,512]{2,1,0:T(4,128)S(1)}, u32[]{:S(2)}, u32[]{:S(2)}) %collective-permute-start.15) | collective-permute-done | bytes 65568 | tf_op jit(solution)/shard_map/ppermute | solution.py:434
  101.6 3.2 %shard_map.161 = (f32[6,6,4,384]{3,2,1,0:T(4,128)}, f32[6,2,2,128]{3,2,1,0:T(2,128)}) custom-call(f32[3,6,4,512]{3,2,1,0:T(4,128)S(1)} %get-tuple-element.66.fv, f32[3,2,2,256]{3,2,1,0:T(2,128)S(1)} %get-tuple-element.67.cv, f32[6,6,4,512]{3,2,1,0:T(4,128)S(1)} %get-tuple-element.59.fs, f32[6,2,2,256]{3,2,1,0:T(2,128)S(1)} %get-tuple-element.60.cs, ...), custom_call_target="tpu_custom_call" | custom-call | flops 10000000 | bytes 10000000 | tf_op jit(solution)/shard_map/pallas_call | solution.py:417
  (44 shorter events, 4.5 us)
Async XLA Ops:
  0.6 19.7 %copy-start.11 = (s32[2,2,128]{2,1,0:T(2,128)S(1)}, s32[2,2,128]{2,1,0:T(2,128)}, u32[]{:S(2)}) copy-start(s32[2,2,128]{2,1,0:T(2,128)} %czone.3) | copy-start | bytes 6148
  0.6 19.7 %copy-start.9 = (f32[3,2,2,128]{3,2,1,0:T(2,128)S(1)}, f32[3,2,2,128]{3,2,1,0:T(2,128)}, u32[]{:S(2)}) copy-start(f32[3,2,2,128]{3,2,1,0:T(2,128)} %cv.3) | copy-start | bytes 18436
  0.7 39.4 %copy-start.12 = (f32[16]{0:T(128)S(1)}, f32[16]{0:T(128)}, u32[]{:S(2)}) copy-start(f32[16]{0:T(128)} %table.3) | copy-start | bytes 196
  0.7 58.2 %copy-start.13 = (f32[16]{0:T(128)S(1)}, f32[16]{0:T(128)}, u32[]{:S(2)}) copy-start(f32[16]{0:T(128)} %rest_0_.1) | copy-start | bytes 196
  0.7 1.6 %copy-start = (f32[10,6,4,6,384]{4,2,3,1,0:T(4,128)S(1)}, f32[10,6,4,6,384]{4,2,3,1,0:T(4,128)}, u32[]{:S(2)}) copy-start(f32[10,6,4,6,384]{4,2,3,1,0:T(4,128)} %param.17) | copy-start | bytes 6635524
  2.3 0.9 copy-start.2
  3.3 0.9 copy-start.3
  4.2 0.8 copy-start.4
  4.9 0.8 copy-start.5
  7.8 12.6 %copy-start.7 = (f32[6,2,2,128]{3,2,1,0:T(2,128)S(1)}, f32[6,2,2,128]{3,2,1,0:T(2,128)}, u32[]{:S(2)}) copy-start(f32[6,2,2,128]{3,2,1,0:T(2,128)} %cs.3) | copy-start | bytes 36868
  7.8 51.1 %copy-start.1 = (f32[10,6,4,6,384]{4,2,3,1,0:T(4,128)S(1)}, f32[10,6,4,6,384]{4,2,3,1,0:T(4,128)}, u32[]{:S(2)}) copy-start(f32[10,6,4,6,384]{4,2,3,1,0:T(4,128)} %param.17) | copy-start | bytes 6635524
  7.8 51.1 %copy-start.14 = (f32[16]{0:T(128)S(1)}, f32[16]{0:T(128)}, u32[]{:S(2)}) copy-start(f32[16]{0:T(128)} %rest_1_.1) | copy-start | bytes 196
  7.8 51.1 %copy-start.15 = (f32[10]{0:T(128)S(1)}, f32[10]{0:T(128)}, u32[]{:S(2)}) copy-start(f32[10]{0:T(128)} %rest_2_.3) | copy-start | bytes 124
  7.8 51.1 %copy-start.16 = (f32[10]{0:T(128)S(1)}, f32[10]{0:T(128)}, u32[]{:S(2)}) copy-start(f32[10]{0:T(128)} %rest_3_.3) | copy-start | bytes 124
  8.3 6.9 %collective-permute-start = (f32[56,4,128]{2,1,0:T(4,128)S(1)}, f32[56,4,128]{2,1,0:T(4,128)S(1)}, u32[]{:S(2)}, u32[]{:S(2)}) collective-permute-start(f32[56,4,128]{2,1,0:T(4,128)S(1)} %get-tuple-element.40), channel_id=1, source_target_pairs={{0,1},{1,2},{2,3},{3,4},{4,5},{5,6},{6,7},{8,9},{9,10},{10,11},{11... | collective-permute-start | bytes 344072 | tf_op jit(solution)/shard_map/ppermute | solution.py:433
  11.6 8.8 %collective-permute-start.1 = (f32[56,4,128]{2,1,0:T(4,128)S(1)}, f32[56,4,128]{2,1,0:T(4,128)S(1)}, u32[]{:S(2)}, u32[]{:S(2)}) collective-permute-start(f32[56,4,128]{2,1,0:T(4,128)S(1)} %get-tuple-element.41), channel_id=1, source_target_pairs={{1,0},{2,1},{3,2},{4,3},{5,4},{6,5},{7,6},{9,8},{10,9},{11,10},{12... | collective-permute-start | bytes 344072 | tf_op jit(solution)/shard_map/ppermute | solution.py:434
  20.5 19.5 %collective-permute-start.4 = (f32[11,4,512]{2,1,0:T(4,128)S(1)}, f32[11,4,512]{2,1,0:T(4,128)S(1)}, u32[]{:S(2)}, u32[]{:S(2)}) collective-permute-start(f32[11,4,512]{2,1,0:T(4,128)S(1)} %get-tuple-element.50), channel_id=1, source_target_pairs={{0,256},{256,512},{512,768},{1,257},{257,513},{513,769},{2,258},{2... | collective-permute-start | bytes 270344 | tf_op jit(solution)/shard_map/ppermute | solution.py:433
  22.5 17.6 %collective-permute-start.5 = (f32[11,4,512]{2,1,0:T(4,128)S(1)}, f32[11,4,512]{2,1,0:T(4,128)S(1)}, u32[]{:S(2)}, u32[]{:S(2)}) collective-permute-start(f32[11,4,512]{2,1,0:T(4,128)S(1)} %get-tuple-element.51), channel_id=1, source_target_pairs={{256,0},{512,256},{768,512},{257,1},{513,257},{769,513},{258,2},{5... | collective-permute-start | bytes 270344 | tf_op jit(solution)/shard_map/ppermute | solution.py:434
  27.6 7.0 %collective-permute-start.2 = (f32[8,4,512]{2,1,0:T(4,128)S(1)}, f32[8,4,512]{2,1,0:T(4,128)S(1)}, u32[]{:S(2)}, u32[]{:S(2)}) collective-permute-start(f32[8,4,512]{2,1,0:T(4,128)S(1)} %get-tuple-element.48), channel_id=1, source_target_pairs={{0,8},{8,16},{16,24},{24,32},{32,40},{40,48},{48,56},{56,64},{64,7... | collective-permute-start | bytes 196616 | tf_op jit(solution)/shard_map/ppermute | solution.py:433
  32.7 7.4 %collective-permute-start.3 = (f32[8,4,512]{2,1,0:T(4,128)S(1)}, f32[8,4,512]{2,1,0:T(4,128)S(1)}, u32[]{:S(2)}, u32[]{:S(2)}) collective-permute-start(f32[8,4,512]{2,1,0:T(4,128)S(1)} %get-tuple-element.49), channel_id=1, source_target_pairs={{8,0},{16,8},{24,16},{32,24},{40,32},{48,40},{56,48},{64,56},{72,6... | collective-permute-start | bytes 196616 | tf_op jit(solution)/shard_map/ppermute | solution.py:434
  41.8 17.1 %collective-permute-start.8 = (f32[11,4,512]{2,1,0:T(4,128)S(1)}, f32[11,4,512]{2,1,0:T(4,128)S(1)}, u32[]{:S(2)}, u32[]{:S(2)}) collective-permute-start(f32[11,4,512]{2,1,0:T(4,128)S(1)} %get-tuple-element.57), channel_id=1, source_target_pairs={{0,256},{256,512},{512,768},{1,257},{257,513},{513,769},{2,258},{2... | collective-permute-start | bytes 270344 | tf_op jit(solution)/shard_map/ppermute | solution.py:433
  43.7 15.2 %collective-permute-start.9 = (f32[11,4,512]{2,1,0:T(4,128)S(1)}, f32[11,4,512]{2,1,0:T(4,128)S(1)}, u32[]{:S(2)}, u32[]{:S(2)}) collective-permute-start(f32[11,4,512]{2,1,0:T(4,128)S(1)} %get-tuple-element.58), channel_id=1, source_target_pairs={{256,0},{512,256},{768,512},{257,1},{513,257},{769,513},{258,2},{5... | collective-permute-start | bytes 270344 | tf_op jit(solution)/shard_map/ppermute | solution.py:434
  48.9 6.2 %collective-permute-start.6 = (f32[8,4,512]{2,1,0:T(4,128)S(1)}, f32[8,4,512]{2,1,0:T(4,128)S(1)}, u32[]{:S(2)}, u32[]{:S(2)}) collective-permute-start(f32[8,4,512]{2,1,0:T(4,128)S(1)} %get-tuple-element.55), channel_id=1, source_target_pairs={{0,8},{8,16},{16,24},{24,32},{32,40},{40,48},{48,56},{56,64},{64,7... | collective-permute-start | bytes 196616 | tf_op jit(solution)/shard_map/ppermute | solution.py:433
  51.5 7.4 %collective-permute-start.7 = (f32[8,4,512]{2,1,0:T(4,128)S(1)}, f32[8,4,512]{2,1,0:T(4,128)S(1)}, u32[]{:S(2)}, u32[]{:S(2)}) collective-permute-start(f32[8,4,512]{2,1,0:T(4,128)S(1)} %get-tuple-element.56), channel_id=1, source_target_pairs={{8,0},{16,8},{24,16},{32,24},{40,32},{48,40},{56,48},{64,56},{72,6... | collective-permute-start | bytes 196616 | tf_op jit(solution)/shard_map/ppermute | solution.py:434
  62.7 18.1 %collective-permute-start.12 = (f32[11,4,512]{2,1,0:T(4,128)S(1)}, f32[11,4,512]{2,1,0:T(4,128)S(1)}, u32[]{:S(2)}, u32[]{:S(2)}) collective-permute-start(f32[11,4,512]{2,1,0:T(4,128)S(1)} %get-tuple-element.63), channel_id=1, source_target_pairs={{0,256},{256,512},{512,768},{1,257},{257,513},{513,769},{2,258},{2... | collective-permute-start | bytes 270344 | tf_op jit(solution)/shard_map/ppermute | solution.py:433
  64.7 16.2 %collective-permute-start.13 = (f32[11,4,512]{2,1,0:T(4,128)S(1)}, f32[11,4,512]{2,1,0:T(4,128)S(1)}, u32[]{:S(2)}, u32[]{:S(2)}) collective-permute-start(f32[11,4,512]{2,1,0:T(4,128)S(1)} %get-tuple-element.64), channel_id=1, source_target_pairs={{256,0},{512,256},{768,512},{257,1},{513,257},{769,513},{258,2},{5... | collective-permute-start | bytes 270344 | tf_op jit(solution)/shard_map/ppermute | solution.py:434
  69.8 6.2 %collective-permute-start.10 = (f32[8,4,512]{2,1,0:T(4,128)S(1)}, f32[8,4,512]{2,1,0:T(4,128)S(1)}, u32[]{:S(2)}, u32[]{:S(2)}) collective-permute-start(f32[8,4,512]{2,1,0:T(4,128)S(1)} %get-tuple-element.61), channel_id=1, source_target_pairs={{0,8},{8,16},{16,24},{24,32},{32,40},{40,48},{48,56},{56,64},{64,7... | collective-permute-start | bytes 196616 | tf_op jit(solution)/shard_map/ppermute | solution.py:433
  73.5 7.4 %collective-permute-start.11 = (f32[8,4,512]{2,1,0:T(4,128)S(1)}, f32[8,4,512]{2,1,0:T(4,128)S(1)}, u32[]{:S(2)}, u32[]{:S(2)}) collective-permute-start(f32[8,4,512]{2,1,0:T(4,128)S(1)} %get-tuple-element.62), channel_id=1, source_target_pairs={{8,0},{16,8},{24,16},{32,24},{40,32},{48,40},{56,48},{64,56},{72,6... | collective-permute-start | bytes 196616 | tf_op jit(solution)/shard_map/ppermute | solution.py:434
  83.2 18.4 %collective-permute-start.16 = (f32[11,4,512]{2,1,0:T(4,128)S(1)}, f32[11,4,512]{2,1,0:T(4,128)S(1)}, u32[]{:S(2)}, u32[]{:S(2)}) collective-permute-start(f32[11,4,512]{2,1,0:T(4,128)S(1)} %get-tuple-element.71), channel_id=1, source_target_pairs={{0,256},{256,512},{512,768},{1,257},{257,513},{513,769},{2,258},{2... | collective-permute-start | bytes 270344 | tf_op jit(solution)/shard_map/ppermute | solution.py:433
  85.1 16.5 %collective-permute-start.17 = (f32[11,4,512]{2,1,0:T(4,128)S(1)}, f32[11,4,512]{2,1,0:T(4,128)S(1)}, u32[]{:S(2)}, u32[]{:S(2)}) collective-permute-start(f32[11,4,512]{2,1,0:T(4,128)S(1)} %get-tuple-element.72), channel_id=1, source_target_pairs={{256,0},{512,256},{768,512},{257,1},{513,257},{769,513},{258,2},{5... | collective-permute-start | bytes 270344 | tf_op jit(solution)/shard_map/ppermute | solution.py:434
  90.3 6.2 %collective-permute-start.14 = (f32[8,4,512]{2,1,0:T(4,128)S(1)}, f32[8,4,512]{2,1,0:T(4,128)S(1)}, u32[]{:S(2)}, u32[]{:S(2)}) collective-permute-start(f32[8,4,512]{2,1,0:T(4,128)S(1)} %get-tuple-element.69), channel_id=1, source_target_pairs={{0,8},{8,16},{16,24},{24,32},{32,40},{40,48},{48,56},{56,64},{64,7... | collective-permute-start | bytes 196616 | tf_op jit(solution)/shard_map/ppermute | solution.py:433
  94.2 7.4 %collective-permute-start.15 = (f32[8,4,512]{2,1,0:T(4,128)S(1)}, f32[8,4,512]{2,1,0:T(4,128)S(1)}, u32[]{:S(2)}, u32[]{:S(2)}) collective-permute-start(f32[8,4,512]{2,1,0:T(4,128)S(1)} %get-tuple-element.70), channel_id=1, source_target_pairs={{8,0},{16,8},{24,16},{32,24},{40,32},{48,40},{56,48},{64,56},{72,6... | collective-permute-start | bytes 196616 | tf_op jit(solution)/shard_map/ppermute | solution.py:434
  (3 other events, 2.1 us)

commit v2 on v1

--- a/solution.py
+++ b/solution.py
@@ -73,7 +73,14 @@
     return roll(tile, -(2 * width * slot + width), 1)
 
 
-def pack_kernel(fs, fv, zone, plastic, states, cs, cv, czone, back, on):
+def pack_kernel(*refs):
+    given, (back, on), held, arrived = refs[:8], refs[8:10], refs[10:18], refs[18]
+    copies = [pltpu.make_async_copy(a, b, arrived.at[i]) for i, (a, b) in enumerate(zip(given, held))]
+    for copy in copies:
+        copy.start()
+    for copy in copies:
+        copy.wait()
+    states, fs, fv, zone, plastic, cs, cv, czone = held
     for way, out in ((0, back), (1, on)):
         lanes = slice(0, TILE) if way == 0 else slice(OWN - TILE, OWN)
 
@@ -437,7 +444,17 @@
 
 def per_device(fv, fs, cv, cs, states, zone, czone, plastic, buoyancy, lame, shear, share, radius):
     fv, fs, states, zone, plastic = [jnp.swapaxes(a, -3, -2) for a in (fv, fs, states, zone, plastic)]
-    sent = call(pack_kernel, [fs, fv, zone, plastic, states, cs, cv, czone], [], [], [Y_MESSAGE] * 2, 0, 10**6)
+    given = [states, fs, fv, zone, plastic, cs, cv, czone]
+    sent = pl.pallas_call(
+        pack_kernel,
+        out_shape=[jax.ShapeDtypeStruct(Y_MESSAGE, F32)] * 2,
+        in_specs=[pl.BlockSpec(memory_space=pltpu.HBM)] * len(given),
+        out_specs=[VMEM] * 2,
+        scratch_shapes=[pltpu.VMEM(a.shape, a.dtype) for a in given]
+        + [pltpu.SemaphoreType.DMA((len(given),))],
+        compiler_params=pltpu.CompilerParams(vmem_limit_bytes=60 * 2**20),
+        cost_estimate=pl.CostEstimate(flops=10**6, bytes_accessed=10**6, transcendentals=0),
+    )(*given)
     y_halo = exchange(["hy"], sent)
     grown = [(6, NX, 4, WIDE), (3, NX, 4, WIDE), (NX, 4, WIDE), (NX, 4, WIDE)]
     grown += [(6, 2, 2, CWIDE), (3, 2, 2, CWIDE), (2, 2, CWIDE)]

time: 106 us -> 101 us (0.953)
  local copies, waits for them, and re-layouts: 7.12 us -> 0.05 us
  Pallas kernels: 11.8 us -> 14.3 us
    unnamed x34 -> x26, local copies, waits for them, and re-layouts: 7.12 us -> 0.05 us
    pallas_call x0 -> x1, Pallas kernels: none -> 3.03 us  [per_device(): pl.pallas_call(pack_kernel, out_shape=[jax.ShapeDtypeStruct(Y_MESSAGE, F3...]
    pallas_call x6 -> x5, Pallas kernels: 11.8 us -> 11.2 us  [call(): pl.pallas_call(body, out_shape=[jax.ShapeDtypeStruct(s, F32) for s in out...]
where the time goes in v2:
time: 101 us; the launch traced here: 100 us
  starting transfers between devices  58.6 us (58%)
  waiting for transfers between devices  26.4 us (26%)
  Pallas kernels  14.3 us (14%)
    ppermute x9, starting transfers between devices, exchange(): found.append(lax.ppermute(back, axis, [(b, a) for a, b in up]))  32.6 us
    ppermute x9, starting transfers between devices, exchange(): found.append(lax.ppermute(on, axis, up))  26 us
    ppermute x9, waiting for transfers between devices, exchange(): found.append(lax.ppermute(back, axis, [(b, a) for a, b in up]))  24.4 us
    pallas_call x5, Pallas kernels, call(): pl.pallas_call(body, out_shape=[jax.ShapeDtypeStruct(s, F32) for s in out...  11.2 us
    pallas_call x1, Pallas kernels, per_device(): pl.pallas_call(pack_kernel, out_shape=[jax.ShapeDtypeStruct(Y_MESSAGE, F3...  3.03 us
    ppermute x9, waiting for transfers between devices, exchange(): found.append(lax.ppermute(on, axis, up))  2.05 us
  transfers between devices with their start and end apart: 18, of which 9 were waited for; matrix products, arithmetic and copies ran while one was open for 0% of the time, Pallas kernels for 0%

profile of v2, /device:TPU:374, one launch (start us, length us, event | category | flops | bytes accessed | tf_op | source)
XLA Modules:
  0.0 100.3 jit_solution(6934124086810673181)
XLA Ops:
  0.8 3.0 %shard_map.156 = (f32[56,4,128]{2,1,0:T(4,128)}, f32[56,4,128]{2,1,0:T(4,128)}) custom-call(f32[10,6,6,4,384]{4,3,2,1,0:T(4,128)} %bitcast.7, f32[6,6,4,384]{3,2,1,0:T(4,128)} %bitcast.9, f32[3,6,4,384]{3,2,1,0:T(4,128)} %bitcast.11, s32[6,4,384]{2,1,0:T(4,128)} %bitcast.13, s32[6,4,384]{2,1,0:T(4,128)} %bitcast.15, f32[6,2,2,128]{3,2,1,0:T(2,128)} %cs.1, ...), custom_call_target="tpu_custom_call" | custom-call | flops 1000000 | bytes 1000000 | tf_op jit(solution)/shard_map/pallas_call | solution.py:448
  3.8 3.1 %collective-permute-start = (f32[56,4,128]{2,1,0:T(4,128)}, f32[56,4,128]{2,1,0:T(4,128)S(1)}, u32[]{:S(2)}, u32[]{:S(2)}) collective-permute-start(f32[56,4,128]{2,1,0:T(4,128)} %get-tuple-element.40), channel_id=1, source_target_pairs={{0,1},{1,2},{2,3},{3,4},{4,5},{5,6},{6,7},{8,9},{9,10},{10,11},{11... | collective-permute-start | bytes 344072 | tf_op jit(solution)/shard_map/ppermute | solution.py:440
  6.9 2.7 %collective-permute-start.1 = (f32[56,4,128]{2,1,0:T(4,128)}, f32[56,4,128]{2,1,0:T(4,128)S(1)}, u32[]{:S(2)}, u32[]{:S(2)}) collective-permute-start(f32[56,4,128]{2,1,0:T(4,128)} %get-tuple-element.41), channel_id=1, source_target_pairs={{1,0},{2,1},{3,2},{4,3},{5,4},{6,5},{7,6},{9,8},{10,9},{11,10},{12... | collective-permute-start | bytes 344072 | tf_op jit(solution)/shard_map/ppermute | solution.py:441
  9.7 1.1 %collective-permute-done.before.rest_0_ = f32[56,4,128]{2,1,0:T(4,128)S(1)} collective-permute-done((f32[56,4,128]{2,1,0:T(4,128)}, f32[56,4,128]{2,1,0:T(4,128)S(1)}, u32[]{:S(2)}, u32[]{:S(2)}) %collective-permute-start) | collective-permute-done | bytes 114720 | tf_op jit(solution)/shard_map/ppermute | solution.py:440
  10.8 5.1 %collective-permute-done.1.after.rest_1_ = f32[56,4,128]{2,1,0:T(4,128)S(1)} collective-permute-done((f32[56,4,128]{2,1,0:T(4,128)}, f32[56,4,128]{2,1,0:T(4,128)S(1)}, u32[]{:S(2)}, u32[]{:S(2)}) %collective-permute-start.1) | collective-permute-done | bytes 114720 | tf_op jit(solution)/shard_map/ppermute | solution.py:441
  16.1 1.9 %collective-permute-start.4 = (f32[11,4,512]{2,1,0:T(4,128)S(1)}, f32[11,4,512]{2,1,0:T(4,128)S(1)}, u32[]{:S(2)}, u32[]{:S(2)}) collective-permute-start(f32[11,4,512]{2,1,0:T(4,128)S(1)} %get-tuple-element.50), channel_id=1, source_target_pairs={{0,256},{256,512},{512,768},{1,257},{257,513},{513,769},{2,258},{2... | collective-permute-start | bytes 270344 | tf_op jit(solution)/shard_map/ppermute | solution.py:440
  18.1 5.1 %collective-permute-start.5 = (f32[11,4,512]{2,1,0:T(4,128)S(1)}, f32[11,4,512]{2,1,0:T(4,128)S(1)}, u32[]{:S(2)}, u32[]{:S(2)}) collective-permute-start(f32[11,4,512]{2,1,0:T(4,128)S(1)} %get-tuple-element.51), channel_id=1, source_target_pairs={{256,0},{512,256},{768,512},{257,1},{513,257},{769,513},{258,2},{5... | collective-permute-start | bytes 270344 | tf_op jit(solution)/shard_map/ppermute | solution.py:441
  23.2 5.0 %collective-permute-start.2 = (f32[8,4,512]{2,1,0:T(4,128)S(1)}, f32[8,4,512]{2,1,0:T(4,128)S(1)}, u32[]{:S(2)}, u32[]{:S(2)}) collective-permute-start(f32[8,4,512]{2,1,0:T(4,128)S(1)} %get-tuple-element.48), channel_id=1, source_target_pairs={{0,8},{8,16},{16,24},{24,32},{32,40},{40,48},{48,56},{56,64},{64,7... | collective-permute-start | bytes 196616 | tf_op jit(solution)/shard_map/ppermute | solution.py:440
  28.3 1.9 %collective-permute-start.3 = (f32[8,4,512]{2,1,0:T(4,128)S(1)}, f32[8,4,512]{2,1,0:T(4,128)S(1)}, u32[]{:S(2)}, u32[]{:S(2)}) collective-permute-start(f32[8,4,512]{2,1,0:T(4,128)S(1)} %get-tuple-element.49), channel_id=1, source_target_pairs={{8,0},{16,8},{24,16},{32,24},{40,32},{48,40},{56,48},{64,56},{72,6... | collective-permute-start | bytes 196616 | tf_op jit(solution)/shard_map/ppermute | solution.py:441
  30.2 5.4 %collective-permute-done.3.rest_1_ = f32[8,4,512]{2,1,0:T(4,128)S(1)} collective-permute-done((f32[8,4,512]{2,1,0:T(4,128)S(1)}, f32[8,4,512]{2,1,0:T(4,128)S(1)}, u32[]{:S(2)}, u32[]{:S(2)}) %collective-permute-start.3) | collective-permute-done | bytes 65568 | tf_op jit(solution)/shard_map/ppermute | solution.py:441
  35.6 1.7 %shard_map.158 = (f32[3,6,4,512]{3,2,1,0:T(4,128)S(1)}, f32[3,2,2,256]{3,2,1,0:T(2,128)S(1)}, f32[8,4,512]{2,1,0:T(4,128)S(1)}, f32[8,4,512]{2,1,0:T(4,128)S(1)}...) custom-call(f32[3,6,4,512]{3,2,1,0:T(4,128)S(1)} %get-tuple-element.42.fv, ...), custom_call_target="tpu_custom_call" | custom-call | flops 1000000 | bytes 1000000 | tf_op jit(solution)/shard_map/pallas_call | solution.py:424
  37.4 1.9 %collective-permute-start.8 = (f32[11,4,512]{2,1,0:T(4,128)S(1)}, f32[11,4,512]{2,1,0:T(4,128)S(1)}, u32[]{:S(2)}, u32[]{:S(2)}) collective-permute-start(f32[11,4,512]{2,1,0:T(4,128)S(1)} %get-tuple-element.57), channel_id=1, source_target_pairs={{0,256},{256,512},{512,768},{1,257},{257,513},{513,769},{2,258},{2... | collective-permute-start | bytes 270344 | tf_op jit(solution)/shard_map/ppermute | solution.py:440
  39.3 5.1 %collective-permute-start.9 = (f32[11,4,512]{2,1,0:T(4,128)S(1)}, f32[11,4,512]{2,1,0:T(4,128)S(1)}, u32[]{:S(2)}, u32[]{:S(2)}) collective-permute-start(f32[11,4,512]{2,1,0:T(4,128)S(1)} %get-tuple-element.58), channel_id=1, source_target_pairs={{256,0},{512,256},{768,512},{257,1},{513,257},{769,513},{258,2},{5... | collective-permute-start | bytes 270344 | tf_op jit(solution)/shard_map/ppermute | solution.py:441
  44.5 2.6 %collective-permute-start.6 = (f32[8,4,512]{2,1,0:T(4,128)S(1)}, f32[8,4,512]{2,1,0:T(4,128)S(1)}, u32[]{:S(2)}, u32[]{:S(2)}) collective-permute-start(f32[8,4,512]{2,1,0:T(4,128)S(1)} %get-tuple-element.55), channel_id=1, source_target_pairs={{0,8},{8,16},{16,24},{24,32},{32,40},{40,48},{48,56},{56,64},{64,7... | collective-permute-start | bytes 196616 | tf_op jit(solution)/shard_map/ppermute | solution.py:440
  47.1 3.2 %collective-permute-start.7 = (f32[8,4,512]{2,1,0:T(4,128)S(1)}, f32[8,4,512]{2,1,0:T(4,128)S(1)}, u32[]{:S(2)}, u32[]{:S(2)}) collective-permute-start(f32[8,4,512]{2,1,0:T(4,128)S(1)} %get-tuple-element.56), channel_id=1, source_target_pairs={{8,0},{16,8},{24,16},{32,24},{40,32},{48,40},{56,48},{64,56},{72,6... | collective-permute-start | bytes 196616 | tf_op jit(solution)/shard_map/ppermute | solution.py:441
  50.3 0.3 collective-permute-done.6.rest_6_
  50.6 3.8 %collective-permute-done.7.rest_7_ = f32[8,4,512]{2,1,0:T(4,128)S(1)} collective-permute-done((f32[8,4,512]{2,1,0:T(4,128)S(1)}, f32[8,4,512]{2,1,0:T(4,128)S(1)}, u32[]{:S(2)}, u32[]{:S(2)}) %collective-permute-start.7) | collective-permute-done | bytes 65568 | tf_op jit(solution)/shard_map/ppermute | solution.py:441
  54.5 3.8 %shard_map.159 = (f32[6,6,4,512]{3,2,1,0:T(4,128)S(1)}, f32[6,2,2,256]{3,2,1,0:T(2,128)S(1)}, f32[10,6,6,4,384]{4,3,2,1,0:T(4,128)S(1)}, f32[8,4,512]{2,1,0:T(4,...) custom-call(f32[3,6,4,512]{3,2,1,0:T(4,128)S(1)} %get-tuple-element.52.fv, ...), custom_call_target="tpu_custom_call" | custom-call | flops 10000000 | bytes 10000000 | tf_op jit(solution)/shard_map/pallas_call | solution.py:424
  58.3 1.9 %collective-permute-start.12 = (f32[11,4,512]{2,1,0:T(4,128)S(1)}, f32[11,4,512]{2,1,0:T(4,128)S(1)}, u32[]{:S(2)}, u32[]{:S(2)}) collective-permute-start(f32[11,4,512]{2,1,0:T(4,128)S(1)} %get-tuple-element.63), channel_id=1, source_target_pairs={{0,256},{256,512},{512,768},{1,257},{257,513},{513,769},{2,258},{2... | collective-permute-start | bytes 270344 | tf_op jit(solution)/shard_map/ppermute | solution.py:440
  60.3 5.1 %collective-permute-start.13 = (f32[11,4,512]{2,1,0:T(4,128)S(1)}, f32[11,4,512]{2,1,0:T(4,128)S(1)}, u32[]{:S(2)}, u32[]{:S(2)}) collective-permute-start(f32[11,4,512]{2,1,0:T(4,128)S(1)} %get-tuple-element.64), channel_id=1, source_target_pairs={{256,0},{512,256},{768,512},{257,1},{513,257},{769,513},{258,2},{5... | collective-permute-start | bytes 270344 | tf_op jit(solution)/shard_map/ppermute | solution.py:441
  65.4 3.6 %collective-permute-start.10 = (f32[8,4,512]{2,1,0:T(4,128)S(1)}, f32[8,4,512]{2,1,0:T(4,128)S(1)}, u32[]{:S(2)}, u32[]{:S(2)}) collective-permute-start(f32[8,4,512]{2,1,0:T(4,128)S(1)} %get-tuple-element.61), channel_id=1, source_target_pairs={{0,8},{8,16},{16,24},{24,32},{32,40},{40,48},{48,56},{56,64},{64,7... | collective-permute-start | bytes 196616 | tf_op jit(solution)/shard_map/ppermute | solution.py:440
  69.1 2.2 %collective-permute-start.11 = (f32[8,4,512]{2,1,0:T(4,128)S(1)}, f32[8,4,512]{2,1,0:T(4,128)S(1)}, u32[]{:S(2)}, u32[]{:S(2)}) collective-permute-start(f32[8,4,512]{2,1,0:T(4,128)S(1)} %get-tuple-element.62), channel_id=1, source_target_pairs={{8,0},{16,8},{24,16},{32,24},{40,32},{48,40},{56,48},{64,56},{72,6... | collective-permute-start | bytes 196616 | tf_op jit(solution)/shard_map/ppermute | solution.py:441
  71.3 0.3 collective-permute-done.10.rest_0_
  71.6 4.9 %collective-permute-done.11.rest_1_ = f32[8,4,512]{2,1,0:T(4,128)S(1)} collective-permute-done((f32[8,4,512]{2,1,0:T(4,128)S(1)}, f32[8,4,512]{2,1,0:T(4,128)S(1)}, u32[]{:S(2)}, u32[]{:S(2)}) %collective-permute-start.11) | collective-permute-done | bytes 65568 | tf_op jit(solution)/shard_map/ppermute | solution.py:441
  76.4 2.3 %shard_map.160 = (f32[3,6,4,512]{3,2,1,0:T(4,128)S(1)}, f32[3,2,2,256]{3,2,1,0:T(2,128)S(1)}, f32[8,4,512]{2,1,0:T(4,128)S(1)}, f32[8,4,512]{2,1,0:T(4,128)S(1)}...) custom-call(f32[3,6,4,512]{3,2,1,0:T(4,128)S(1)} %get-tuple-element., ...), custom_call_target="tpu_custom_call" | custom-call | flops 1000000 | bytes 1000000 | tf_op jit(solution)/shard_map/pallas_call | solution.py:424
  78.8 1.9 %collective-permute-start.16 = (f32[11,4,512]{2,1,0:T(4,128)S(1)}, f32[11,4,512]{2,1,0:T(4,128)S(1)}, u32[]{:S(2)}, u32[]{:S(2)}) collective-permute-start(f32[11,4,512]{2,1,0:T(4,128)S(1)} %get-tuple-element.71), channel_id=1, source_target_pairs={{0,256},{256,512},{512,768},{1,257},{257,513},{513,769},{2,258},{2... | collective-permute-start | bytes 270344 | tf_op jit(solution)/shard_map/ppermute | solution.py:440
  80.7 5.1 %collective-permute-start.17 = (f32[11,4,512]{2,1,0:T(4,128)S(1)}, f32[11,4,512]{2,1,0:T(4,128)S(1)}, u32[]{:S(2)}, u32[]{:S(2)}) collective-permute-start(f32[11,4,512]{2,1,0:T(4,128)S(1)} %get-tuple-element.72), channel_id=1, source_target_pairs={{256,0},{512,256},{768,512},{257,1},{513,257},{769,513},{258,2},{5... | collective-permute-start | bytes 270344 | tf_op jit(solution)/shard_map/ppermute | solution.py:441
  85.8 3.9 %collective-permute-start.14 = (f32[8,4,512]{2,1,0:T(4,128)S(1)}, f32[8,4,512]{2,1,0:T(4,128)S(1)}, u32[]{:S(2)}, u32[]{:S(2)}) collective-permute-start(f32[8,4,512]{2,1,0:T(4,128)S(1)} %get-tuple-element.69), channel_id=1, source_target_pairs={{0,8},{8,16},{16,24},{24,32},{32,40},{40,48},{48,56},{56,64},{64,7... | collective-permute-start | bytes 196616 | tf_op jit(solution)/shard_map/ppermute | solution.py:440
  89.8 1.9 %collective-permute-start.15 = (f32[8,4,512]{2,1,0:T(4,128)S(1)}, f32[8,4,512]{2,1,0:T(4,128)S(1)}, u32[]{:S(2)}, u32[]{:S(2)}) collective-permute-start(f32[8,4,512]{2,1,0:T(4,128)S(1)} %get-tuple-element.70), channel_id=1, source_target_pairs={{8,0},{16,8},{24,16},{32,24},{40,32},{48,40},{56,48},{64,56},{72,6... | collective-permute-start | bytes 196616 | tf_op jit(solution)/shard_map/ppermute | solution.py:441
  91.7 0.3 collective-permute-done.14.rest_4_
  92.0 5.1 %collective-permute-done.15.rest_5_ = f32[8,4,512]{2,1,0:T(4,128)S(1)} collective-permute-done((f32[8,4,512]{2,1,0:T(4,128)S(1)}, f32[8,4,512]{2,1,0:T(4,128)S(1)}, u32[]{:S(2)}, u32[]{:S(2)}) %collective-permute-start.15) | collective-permute-done | bytes 65568 | tf_op jit(solution)/shard_map/ppermute | solution.py:441
  97.1 3.2 %shard_map.161 = (f32[6,6,4,384]{3,2,1,0:T(4,128)}, f32[6,2,2,128]{3,2,1,0:T(2,128)}) custom-call(f32[3,6,4,512]{3,2,1,0:T(4,128)S(1)} %get-tuple-element.66.fv, f32[3,2,2,256]{3,2,1,0:T(2,128)S(1)} %get-tuple-element.67.cv, f32[6,6,4,512]{3,2,1,0:T(4,128)S(1)} %get-tuple-element.59.fs, f32[6,2,2,256]{3,2,1,0:T(2,128)S(1)} %get-tuple-element.60.cs, ...), custom_call_target="tpu_custom_call" | custom-call | flops 10000000 | bytes 10000000 | tf_op jit(solution)/shard_map/pallas_call | solution.py:424
  (36 shorter events, 0.2 us)
Async XLA Ops:
  0.6 15.3 %copy-start.7 = (s32[2,2,128]{2,1,0:T(2,128)S(1)}, s32[2,2,128]{2,1,0:T(2,128)}, u32[]{:S(2)}) copy-start(s32[2,2,128]{2,1,0:T(2,128)} %czone.1) | copy-start | bytes 6148
  0.6 15.3 %copy-start.5 = (f32[6,2,2,128]{3,2,1,0:T(2,128)S(1)}, f32[6,2,2,128]{3,2,1,0:T(2,128)}, u32[]{:S(2)}) copy-start(f32[6,2,2,128]{3,2,1,0:T(2,128)} %cs.1) | copy-start | bytes 36868
  0.7 15.3 %copy-start.6 = (f32[3,2,2,128]{3,2,1,0:T(2,128)S(1)}, f32[3,2,2,128]{3,2,1,0:T(2,128)}, u32[]{:S(2)}) copy-start(f32[3,2,2,128]{3,2,1,0:T(2,128)} %cv.1) | copy-start | bytes 18436
  0.7 15.3 %copy-start.4 = (s32[4,6,384]{2,0,1:T(4,128)S(1)}, s32[4,6,384]{2,0,1:T(4,128)}, u32[]{:S(2)}) copy-start(s32[4,6,384]{2,0,1:T(4,128)} %param.20) | copy-start | bytes 110596
  0.7 15.3 %copy-start.3 = (s32[4,6,384]{2,0,1:T(4,128)S(1)}, s32[4,6,384]{2,0,1:T(4,128)}, u32[]{:S(2)}) copy-start(s32[4,6,384]{2,0,1:T(4,128)} %param.18) | copy-start | bytes 110596
  0.7 53.8 %copy-start = (f32[10,6,4,6,384]{4,2,3,1,0:T(4,128)S(1)}, f32[10,6,4,6,384]{4,2,3,1,0:T(4,128)}, u32[]{:S(2)}) copy-start(f32[10,6,4,6,384]{4,2,3,1,0:T(4,128)} %param.17) | copy-start | bytes 6635524
  0.7 15.3 %copy-start.1 = (f32[6,4,6,384]{3,1,2,0:T(4,128)S(1)}, f32[6,4,6,384]{3,1,2,0:T(4,128)}, u32[]{:S(2)}) copy-start(f32[6,4,6,384]{3,1,2,0:T(4,128)} %param.14) | copy-start | bytes 663556
  0.7 15.3 %copy-start.2 = (f32[3,4,6,384]{3,1,2,0:T(4,128)S(1)}, f32[3,4,6,384]{3,1,2,0:T(4,128)}, u32[]{:S(2)}) copy-start(f32[3,4,6,384]{3,1,2,0:T(4,128)} %param.13) | copy-start | bytes 331780
  0.7 34.9 %copy-start.8 = (f32[16]{0:T(128)S(1)}, f32[16]{0:T(128)}, u32[]{:S(2)}) copy-start(f32[16]{0:T(128)} %table.3) | copy-start | bytes 196
  0.7 53.7 %copy-start.12 = (f32[10]{0:T(128)S(1)}, f32[10]{0:T(128)}, u32[]{:S(2)}) copy-start(f32[10]{0:T(128)} %rest_3_.3) | copy-start | bytes 124
  0.7 53.7 %copy-start.11 = (f32[10]{0:T(128)S(1)}, f32[10]{0:T(128)}, u32[]{:S(2)}) copy-start(f32[10]{0:T(128)} %rest_2_.3) | copy-start | bytes 124
  0.7 53.7 %copy-start.10 = (f32[16]{0:T(128)S(1)}, f32[16]{0:T(128)}, u32[]{:S(2)}) copy-start(f32[16]{0:T(128)} %rest_1_.1) | copy-start | bytes 196
  0.8 53.7 %copy-start.9 = (f32[16]{0:T(128)S(1)}, f32[16]{0:T(128)}, u32[]{:S(2)}) copy-start(f32[16]{0:T(128)} %rest_0_.1) | copy-start | bytes 196
  3.8 7.0 %collective-permute-start = (f32[56,4,128]{2,1,0:T(4,128)}, f32[56,4,128]{2,1,0:T(4,128)S(1)}, u32[]{:S(2)}, u32[]{:S(2)}) collective-permute-start(f32[56,4,128]{2,1,0:T(4,128)} %get-tuple-element.40), channel_id=1, source_target_pairs={{0,1},{1,2},{2,3},{3,4},{4,5},{5,6},{6,7},{8,9},{9,10},{10,11},{11... | collective-permute-start | bytes 344072 | tf_op jit(solution)/shard_map/ppermute | solution.py:440
  6.9 9.0 %collective-permute-start.1 = (f32[56,4,128]{2,1,0:T(4,128)}, f32[56,4,128]{2,1,0:T(4,128)S(1)}, u32[]{:S(2)}, u32[]{:S(2)}) collective-permute-start(f32[56,4,128]{2,1,0:T(4,128)} %get-tuple-element.41), channel_id=1, source_target_pairs={{1,0},{2,1},{3,2},{4,3},{5,4},{6,5},{7,6},{9,8},{10,9},{11,10},{12... | collective-permute-start | bytes 344072 | tf_op jit(solution)/shard_map/ppermute | solution.py:441
  16.1 19.5 %collective-permute-start.4 = (f32[11,4,512]{2,1,0:T(4,128)S(1)}, f32[11,4,512]{2,1,0:T(4,128)S(1)}, u32[]{:S(2)}, u32[]{:S(2)}) collective-permute-start(f32[11,4,512]{2,1,0:T(4,128)S(1)} %get-tuple-element.50), channel_id=1, source_target_pairs={{0,256},{256,512},{512,768},{1,257},{257,513},{513,769},{2,258},{2... | collective-permute-start | bytes 270344 | tf_op jit(solution)/shard_map/ppermute | solution.py:440
  18.1 17.6 %collective-permute-start.5 = (f32[11,4,512]{2,1,0:T(4,128)S(1)}, f32[11,4,512]{2,1,0:T(4,128)S(1)}, u32[]{:S(2)}, u32[]{:S(2)}) collective-permute-start(f32[11,4,512]{2,1,0:T(4,128)S(1)} %get-tuple-element.51), channel_id=1, source_target_pairs={{256,0},{512,256},{768,512},{257,1},{513,257},{769,513},{258,2},{5... | collective-permute-start | bytes 270344 | tf_op jit(solution)/shard_map/ppermute | solution.py:441
  23.2 7.0 %collective-permute-start.2 = (f32[8,4,512]{2,1,0:T(4,128)S(1)}, f32[8,4,512]{2,1,0:T(4,128)S(1)}, u32[]{:S(2)}, u32[]{:S(2)}) collective-permute-start(f32[8,4,512]{2,1,0:T(4,128)S(1)} %get-tuple-element.48), channel_id=1, source_target_pairs={{0,8},{8,16},{16,24},{24,32},{32,40},{40,48},{48,56},{56,64},{64,7... | collective-permute-start | bytes 196616 | tf_op jit(solution)/shard_map/ppermute | solution.py:440
  28.3 7.4 %collective-permute-start.3 = (f32[8,4,512]{2,1,0:T(4,128)S(1)}, f32[8,4,512]{2,1,0:T(4,128)S(1)}, u32[]{:S(2)}, u32[]{:S(2)}) collective-permute-start(f32[8,4,512]{2,1,0:T(4,128)S(1)} %get-tuple-element.49), channel_id=1, source_target_pairs={{8,0},{16,8},{24,16},{32,24},{40,32},{48,40},{56,48},{64,56},{72,6... | collective-permute-start | bytes 196616 | tf_op jit(solution)/shard_map/ppermute | solution.py:441
  37.4 17.1 %collective-permute-start.8 = (f32[11,4,512]{2,1,0:T(4,128)S(1)}, f32[11,4,512]{2,1,0:T(4,128)S(1)}, u32[]{:S(2)}, u32[]{:S(2)}) collective-permute-start(f32[11,4,512]{2,1,0:T(4,128)S(1)} %get-tuple-element.57), channel_id=1, source_target_pairs={{0,256},{256,512},{512,768},{1,257},{257,513},{513,769},{2,258},{2... | collective-permute-start | bytes 270344 | tf_op jit(solution)/shard_map/ppermute | solution.py:440
  39.3 15.2 %collective-permute-start.9 = (f32[11,4,512]{2,1,0:T(4,128)S(1)}, f32[11,4,512]{2,1,0:T(4,128)S(1)}, u32[]{:S(2)}, u32[]{:S(2)}) collective-permute-start(f32[11,4,512]{2,1,0:T(4,128)S(1)} %get-tuple-element.58), channel_id=1, source_target_pairs={{256,0},{512,256},{768,512},{257,1},{513,257},{769,513},{258,2},{5... | collective-permute-start | bytes 270344 | tf_op jit(solution)/shard_map/ppermute | solution.py:441
  44.5 6.2 %collective-permute-start.6 = (f32[8,4,512]{2,1,0:T(4,128)S(1)}, f32[8,4,512]{2,1,0:T(4,128)S(1)}, u32[]{:S(2)}, u32[]{:S(2)}) collective-permute-start(f32[8,4,512]{2,1,0:T(4,128)S(1)} %get-tuple-element.55), channel_id=1, source_target_pairs={{0,8},{8,16},{16,24},{24,32},{32,40},{40,48},{48,56},{56,64},{64,7... | collective-permute-start | bytes 196616 | tf_op jit(solution)/shard_map/ppermute | solution.py:440
  47.1 7.4 %collective-permute-start.7 = (f32[8,4,512]{2,1,0:T(4,128)S(1)}, f32[8,4,512]{2,1,0:T(4,128)S(1)}, u32[]{:S(2)}, u32[]{:S(2)}) collective-permute-start(f32[8,4,512]{2,1,0:T(4,128)S(1)} %get-tuple-element.56), channel_id=1, source_target_pairs={{8,0},{16,8},{24,16},{32,24},{40,32},{48,40},{56,48},{64,56},{72,6... | collective-permute-start | bytes 196616 | tf_op jit(solution)/shard_map/ppermute | solution.py:441
  58.3 18.1 %collective-permute-start.12 = (f32[11,4,512]{2,1,0:T(4,128)S(1)}, f32[11,4,512]{2,1,0:T(4,128)S(1)}, u32[]{:S(2)}, u32[]{:S(2)}) collective-permute-start(f32[11,4,512]{2,1,0:T(4,128)S(1)} %get-tuple-element.63), channel_id=1, source_target_pairs={{0,256},{256,512},{512,768},{1,257},{257,513},{513,769},{2,258},{2... | collective-permute-start | bytes 270344 | tf_op jit(solution)/shard_map/ppermute | solution.py:440
  60.3 16.2 %collective-permute-start.13 = (f32[11,4,512]{2,1,0:T(4,128)S(1)}, f32[11,4,512]{2,1,0:T(4,128)S(1)}, u32[]{:S(2)}, u32[]{:S(2)}) collective-permute-start(f32[11,4,512]{2,1,0:T(4,128)S(1)} %get-tuple-element.64), channel_id=1, source_target_pairs={{256,0},{512,256},{768,512},{257,1},{513,257},{769,513},{258,2},{5... | collective-permute-start | bytes 270344 | tf_op jit(solution)/shard_map/ppermute | solution.py:441
  65.4 6.2 %collective-permute-start.10 = (f32[8,4,512]{2,1,0:T(4,128)S(1)}, f32[8,4,512]{2,1,0:T(4,128)S(1)}, u32[]{:S(2)}, u32[]{:S(2)}) collective-permute-start(f32[8,4,512]{2,1,0:T(4,128)S(1)} %get-tuple-element.61), channel_id=1, source_target_pairs={{0,8},{8,16},{16,24},{24,32},{32,40},{40,48},{48,56},{56,64},{64,7... | collective-permute-start | bytes 196616 | tf_op jit(solution)/shard_map/ppermute | solution.py:440
  69.1 7.4 %collective-permute-start.11 = (f32[8,4,512]{2,1,0:T(4,128)S(1)}, f32[8,4,512]{2,1,0:T(4,128)S(1)}, u32[]{:S(2)}, u32[]{:S(2)}) collective-permute-start(f32[8,4,512]{2,1,0:T(4,128)S(1)} %get-tuple-element.62), channel_id=1, source_target_pairs={{8,0},{16,8},{24,16},{32,24},{40,32},{48,40},{56,48},{64,56},{72,6... | collective-permute-start | bytes 196616 | tf_op jit(solution)/shard_map/ppermute | solution.py:441
  78.8 18.4 %collective-permute-start.16 = (f32[11,4,512]{2,1,0:T(4,128)S(1)}, f32[11,4,512]{2,1,0:T(4,128)S(1)}, u32[]{:S(2)}, u32[]{:S(2)}) collective-permute-start(f32[11,4,512]{2,1,0:T(4,128)S(1)} %get-tuple-element.71), channel_id=1, source_target_pairs={{0,256},{256,512},{512,768},{1,257},{257,513},{513,769},{2,258},{2... | collective-permute-start | bytes 270344 | tf_op jit(solution)/shard_map/ppermute | solution.py:440
  80.7 16.5 %collective-permute-start.17 = (f32[11,4,512]{2,1,0:T(4,128)S(1)}, f32[11,4,512]{2,1,0:T(4,128)S(1)}, u32[]{:S(2)}, u32[]{:S(2)}) collective-permute-start(f32[11,4,512]{2,1,0:T(4,128)S(1)} %get-tuple-element.72), channel_id=1, source_target_pairs={{256,0},{512,256},{768,512},{257,1},{513,257},{769,513},{258,2},{5... | collective-permute-start | bytes 270344 | tf_op jit(solution)/shard_map/ppermute | solution.py:441
  85.8 6.2 %collective-permute-start.14 = (f32[8,4,512]{2,1,0:T(4,128)S(1)}, f32[8,4,512]{2,1,0:T(4,128)S(1)}, u32[]{:S(2)}, u32[]{:S(2)}) collective-permute-start(f32[8,4,512]{2,1,0:T(4,128)S(1)} %get-tuple-element.69), channel_id=1, source_target_pairs={{0,8},{8,16},{16,24},{24,32},{32,40},{40,48},{48,56},{56,64},{64,7... | collective-permute-start | bytes 196616 | tf_op jit(solution)/shard_map/ppermute | solution.py:440
  89.8 7.4 %collective-permute-start.15 = (f32[8,4,512]{2,1,0:T(4,128)S(1)}, f32[8,4,512]{2,1,0:T(4,128)S(1)}, u32[]{:S(2)}, u32[]{:S(2)}) collective-permute-start(f32[8,4,512]{2,1,0:T(4,128)S(1)} %get-tuple-element.70), channel_id=1, source_target_pairs={{8,0},{16,8},{24,16},{32,24},{40,32},{48,40},{56,48},{64,56},{72,6... | collective-permute-start | bytes 196616 | tf_op jit(solution)/shard_map/ppermute | solution.py:441

commit v3 on v2

--- a/solution.py
+++ b/solution.py
@@ -73,11 +73,29 @@
     return roll(tile, -(2 * width * slot + width), 1)
 
 
+def between_grids(shape, wide_axis):
+    wide, narrow = iota(shape, wide_axis), iota(shape, 1 - wide_axis)
+    first = jnp.where(narrow < CWIDE - TILE // 2, narrow, narrow - CWIDE) * 3
+    wide = jnp.where(wide < WIDE - TILE // 2, wide, wide - WIDE)
+    return jnp.where((wide >= first) & (wide < first + 3), 1.0, 0.0).astype(jnp.bfloat16)
+
+
+def in_pieces(x, ones):
+    high = x.astype(jnp.bfloat16).astype(F32)
+    rest = x - high
+    middle = rest.astype(jnp.bfloat16).astype(F32)
+    pieces = jnp.concatenate([high, middle, rest - middle], 0).astype(jnp.bfloat16)
+    out = jnp.dot(pieces, ones, preferred_element_type=F32)
+    return out[0:16] + out[16:32] + out[32:48]
+
+
 def pack_kernel(*refs):
-    given, (back, on), held, arrived = refs[:8], refs[8:10], refs[10:18], refs[18]
+    given, (back, on, repeat, gather), held, arrived = refs[:8], refs[8:12], refs[12:20], refs[20]
     copies = [pltpu.make_async_copy(a, b, arrived.at[i]) for i, (a, b) in enumerate(zip(given, held))]
     for copy in copies:
         copy.start()
+    repeat[...] = between_grids((CWIDE, WIDE), 1)
+    gather[...] = between_grids((WIDE, CWIDE), 0)
     for copy in copies:
         copy.wait()
     states, fs, fv, zone, plastic, cs, cv, czone = held
@@ -177,7 +195,8 @@
 
 
 class Fields:
-    def __init__(self, fine, coarse, sets, halos, rooms):
+    def __init__(self, fine, coarse, sets, maps, halos, rooms):
+        self.repeat, self.gather = maps
         self.fine, self.coarse, self.sets = fine, coarse, sets
         self.x_before, self.x_after, self.z_before, self.z_after = halos
         self.z_room, self.c_room, self.narrow_room, self.wide_room = rooms
@@ -203,19 +222,8 @@
         bottom = (lax.axis_index("depth") == lax.axis_size("depth") - 1).astype(F32)
         comps = self.sets["z"]
 
-        def match(shape, wide_axis):
-            wide, narrow = iota(shape, wide_axis), iota(shape, 1 - wide_axis)
-            first = jnp.where(narrow < CWIDE - TILE // 2, narrow, narrow - CWIDE) * 3
-            wide = jnp.where(wide < WIDE - TILE // 2, wide, wide - WIDE)
-            return (wide >= first) & (wide < first + 3)
-
-        repeat = jnp.where(match((CWIDE, WIDE), 1), 1.0, 0.0).astype(F32)
-        gather = jnp.where(match((WIDE, CWIDE), 0), bottom / 9.0, 0.0).astype(F32)
-        dot = functools.partial(
-            jnp.dot, precision=lax.Precision.HIGHEST, preferred_element_type=F32
-        )
         narrow, wide = self.narrow_room, self.wide_room
-        narrow[6:8] = jnp.zeros((2, CWIDE), F32)
+        narrow[6:16] = jnp.zeros((10, CWIDE), F32)
         wide[12:16] = jnp.zeros((4, WIDE), F32)
         for place, c in enumerate(comps):
             narrow[2 * place : 2 * place + 2] = self.coarse[c, 0]
@@ -224,8 +232,8 @@
                     at = 4 * place + 2 * step + r
                     line = [self.fine[c, 3 * r + i, z : z + 1] for i in range(3)]
                     wide[at : at + 1] = line[0] + line[1] + line[2]
-        spread = dot(narrow[...], repeat)
-        means = dot(wide[...], gather)
+        spread = in_pieces(narrow[...], self.repeat[...])
+        means = in_pieces(wide[...], self.gather[...]) * (bottom / 9.0)
         self.below, self.above = {}, {}
         far = iota((2, WIDE), 0) == 1
         for place, c in enumerate(comps):
@@ -316,36 +324,36 @@
     )
 
 
-def velocity_kernel(last, fv, cv, fs, cs, zone, czone, table, *rest):
+def velocity_kernel(fv, cv, fs, cs, zone, czone, repeat, gather, table, *rest):
     halos, rest = rest[:4], rest[4:]
     nfv, ncv, *out = rest[:6]
-    f = Fields(fs, cs, STRESS, halos, rest[-4:])
+    f = Fields(fs, cs, STRESS, (repeat, gather), halos, rest[-4:])
     for x in range(NX):
         gain = DT * lookup(zone[x], table)
         found = forces(*f.fine_ways(x), 1.0)
         for c in range(3):
-            new = fv[c, x] + gain * found[c]
-            nfv[c, x] = new
-            if last:
-                rest[6][c, x] = new[:, 0:OWN]
+            nfv[c, x] = fv[c, x] + gain * found[c]
     for z in range(2):
         gain = DT * lookup(czone[z], table)
         found = forces(*f.coarse_ways(z), 1.0 / 3.0)
         for c in range(3):
-            new = cv[c, z] + gain * found[c]
-            ncv[c, z] = new
-            if last:
-                rest[7][c, 1 - z] = new[:, 0:TILE]
+            ncv[c, z] = cv[c, z] + gain * found[c]
     pack(nfv, ncv, SPEED, out)
 
 
-def stress_kernel(last, fv, cv, fs, cs, zone, czone, plastic, states, *rest):
+def stress_kernel(last, fv, cv, fs, cs, zone, czone, repeat, gather, plastic, states, *rest):
     before, after = (None, None) if last else rest[:2]
     rest = rest if last else rest[2:]
     lame, shear, share, radius = rest[:4]
     halos, rest = rest[4:8], rest[8:]
     nfs, ncs = rest[:2]
-    f = Fields(fv, cv, SPEED, halos, rest[-4:])
+    f = Fields(fv, cv, SPEED, (repeat, gather), halos, rest[4 if last else 7 :][:4])
+    if last:
+        sending = pltpu.make_async_copy(fv.at[:, :, :, 0:OWN], rest[2], rest[8].at[0])
+        sending.start()
+        for c in range(3):
+            for z in range(2):
+                rest[3][c, 1 - z] = cv[c, z, :, 0:TILE]
     width = OWN if last else WIDE
     total = share[0]
     for k in range(1, share.shape[0]):
@@ -410,7 +418,9 @@
                 ncs[c, 1 - z] = new[:, 0:TILE]
             else:
                 ncs[c, z] = new
-    if not last:
+    if last:
+        sending.wait()
+    else:
         pack(nfs, ncs, STRESS, rest[3:7])
 
 
@@ -419,14 +429,15 @@
 SENT = [X_MESSAGE, X_MESSAGE, Z_MESSAGE, Z_MESSAGE]
 
 
-def call(body, operands, scalars, halos, outs, fields, flops):
-    rooms = [(3, NX, 8, WIDE), (fields, 2, 8, CWIDE), (8, CWIDE), (16, WIDE)] if fields else []
+def call(body, operands, scalars, halos, outs, fields, flops, direct=()):
+    rooms = [(3, NX, 8, WIDE), (fields, 2, 8, CWIDE), (16, CWIDE), (16, WIDE)] if fields else []
     return pl.pallas_call(
         body,
         out_shape=[jax.ShapeDtypeStruct(s, F32) for s in outs],
         in_specs=[VMEM] * len(operands) + [SMEM] * len(scalars) + [VMEM] * len(halos),
-        out_specs=[VMEM] * len(outs),
-        scratch_shapes=[pltpu.VMEM(s, F32) for s in rooms],
+        out_specs=[pl.BlockSpec(memory_space=pltpu.HBM) if i in direct else VMEM for i in range(len(outs))],
+        scratch_shapes=[pltpu.VMEM(s, F32) for s in rooms]
+        + ([pltpu.SemaphoreType.DMA((len(direct),))] if direct else []),
         compiler_params=pltpu.CompilerParams(vmem_limit_bytes=40 * 2**20),
         cost_estimate=pl.CostEstimate(flops=flops, bytes_accessed=flops, transcendentals=0),
     )(*operands, *scalars, *halos)
@@ -445,11 +456,12 @@
 def per_device(fv, fs, cv, cs, states, zone, czone, plastic, buoyancy, lame, shear, share, radius):
     fv, fs, states, zone, plastic = [jnp.swapaxes(a, -3, -2) for a in (fv, fs, states, zone, plastic)]
     given = [states, fs, fv, zone, plastic, cs, cv, czone]
-    sent = pl.pallas_call(
+    *sent, repeat, gather = pl.pallas_call(
         pack_kernel,
-        out_shape=[jax.ShapeDtypeStruct(Y_MESSAGE, F32)] * 2,
+        out_shape=[jax.ShapeDtypeStruct(Y_MESSAGE, F32)] * 2
+        + [jax.ShapeDtypeStruct(s, jnp.bfloat16) for s in ((CWIDE, WIDE), (WIDE, CWIDE))],
         in_specs=[pl.BlockSpec(memory_space=pltpu.HBM)] * len(given),
-        out_specs=[VMEM] * 2,
+        out_specs=[VMEM] * 4,
         scratch_shapes=[pltpu.VMEM(a.shape, a.dtype) for a in given]
         + [pltpu.SemaphoreType.DMA((len(given),))],
         compiler_params=pltpu.CompilerParams(vmem_limit_bytes=60 * 2**20),
@@ -463,36 +475,34 @@
     )
     for step in range(2):
         last = step == 1
-        outs = [fv.shape, cv.shape] + SENT + ([(3, NX, 4, OWN), (3, 2, 2, TILE)] if last else [])
-        found = call(
-            functools.partial(velocity_kernel, last),
-            [fv, cv, fs, cs, zone, czone],
+        fv, cv, *sent = call(
+            velocity_kernel,
+            [fv, cv, fs, cs, zone, czone, repeat, gather],
             [buoyancy],
             exchange(["hx", "depth"], sent),
-            outs,
+            [fv.shape, cv.shape] + SENT,
             6,
             10**6,
         )
-        fv, cv, *sent = found[:6]
         if last:
-            fv_out, cv_out = found[6:]
-            outs = [(6, NX, 4, OWN), (6, 2, 2, TILE)]
+            outs = [(6, NX, 4, OWN), (6, 2, 2, TILE), (3, NX, 4, OWN), (3, 2, 2, TILE)]
         else:
             outs = [fs.shape, cs.shape, states.shape] + SENT
         found = call(
             functools.partial(stress_kernel, last),
-            [fv, cv, fs, cs, zone, czone, plastic, states] + ([] if last else y_halo),
+            [fv, cv, fs, cs, zone, czone, repeat, gather, plastic, states] + ([] if last else y_halo),
             [lame, shear, share, radius],
             exchange(["hx", "depth"], sent),
             outs,
             3,
             10**7,
+            (2,) if last else (),
         )
         if last:
-            fs, cs = found
+            fs, cs, fv, cv = found
         else:
             fs, cs, states, *sent = found
-    return jnp.swapaxes(fv_out, 1, 2), jnp.swapaxes(fs, 1, 2), cv_out, cs
+    return jnp.swapaxes(fv, 1, 2), jnp.swapaxes(fs, 1, 2), cv, cs
 
 
 def solution(mesh):

time: 101 us -> 101 us (level)
  Pallas kernels: 14.3 us -> 12.3 us
  local copies, waits for them, and re-layouts: 0.05 us -> 1.95 us
    pallas_call x5, Pallas kernels: 11.2 us -> 9.13 us  [call(): pl.pallas_call(body, out_shape=[jax.ShapeDtypeStruct(s, F32) for s in out...]
    unnamed x26 -> x30, local copies, waits for them, and re-layouts: 0.05 us -> 1.95 us
where the time goes in v3:
time: 101 us; the launch traced here: 100 us
  starting transfers between devices  58.6 us (58%)
  waiting for transfers between devices  26.4 us (26%)
  Pallas kernels  12.3 us (12%)
  local copies, waits for them, and re-layouts  1.95 us (2%)
    ppermute x9, starting transfers between devices, exchange(): found.append(lax.ppermute(back, axis, [(b, a) for a, b in up]))  32.6 us
    ppermute x9, starting transfers between devices, exchange(): found.append(lax.ppermute(on, axis, up))  26 us
    ppermute x9, waiting for transfers between devices, exchange(): found.append(lax.ppermute(back, axis, [(b, a) for a, b in up]))  24.4 us
    pallas_call x5, Pallas kernels, call(): pl.pallas_call(body, out_shape=[jax.ShapeDtypeStruct(s, F32) for s in out...  9.13 us
    pallas_call x1, Pallas kernels, per_device(): pl.pallas_call(pack_kernel, out_shape=[jax.ShapeDtypeStruct(Y_MESSAGE, F3...  3.14 us
    ppermute x9, waiting for transfers between devices, exchange(): found.append(lax.ppermute(on, axis, up))  2.05 us
  transfers between devices with their start and end apart: 18, of which 9 were waited for; matrix products, arithmetic and copies ran while one was open for 0% of the time, Pallas kernels for 0%

profile of v3, /device:TPU:374, one launch (start us, length us, event | category | flops | bytes accessed | tf_op | source)
XLA Modules:
  0.0 100.3 jit_solution(3219434596597693598)
XLA Ops:
  0.8 3.1 %shard_map.156 = (f32[56,4,128]{2,1,0:T(4,128)}, f32[56,4,128]{2,1,0:T(4,128)}, bf16[256,512]{1,0:T(8,128)(2,1)}, bf16[512,256]{1,0:T(8,128)(2,1)}) custom-call(f32[10,6,6,4,384]{4,3,2,1,0:T(4,128)} %bitcast.7, f32[6,6,4,384]{3,2,1,0:T(4,128)} %bitcast.9, f32[3,6,4,384]{3,2,1,0:T(4,128)} %bitcast.11, s32[6,4,384]{2,1,0:T(4,128)} %bitcast.13, ...), custom_call_target="tpu_custom_call" | custom-call | flops 1000000 | bytes 1000000 | tf_op jit(solution)/shard_map/pallas_call | solution.py:459
  3.9 3.1 %collective-permute-start = (f32[56,4,128]{2,1,0:T(4,128)}, f32[56,4,128]{2,1,0:T(4,128)S(1)}, u32[]{:S(2)}, u32[]{:S(2)}) collective-permute-start(f32[56,4,128]{2,1,0:T(4,128)} %get-tuple-element.42), channel_id=1, source_target_pairs={{0,1},{1,2},{2,3},{3,4},{4,5},{5,6},{6,7},{8,9},{9,10},{10,11},{11... | collective-permute-start | bytes 344072 | tf_op jit(solution)/shard_map/ppermute | solution.py:451
  7.0 2.7 %collective-permute-start.1 = (f32[56,4,128]{2,1,0:T(4,128)}, f32[56,4,128]{2,1,0:T(4,128)S(1)}, u32[]{:S(2)}, u32[]{:S(2)}) collective-permute-start(f32[56,4,128]{2,1,0:T(4,128)} %get-tuple-element.43), channel_id=1, source_target_pairs={{1,0},{2,1},{3,2},{4,3},{5,4},{6,5},{7,6},{9,8},{10,9},{11,10},{12... | collective-permute-start | bytes 344072 | tf_op jit(solution)/shard_map/ppermute | solution.py:452
  9.8 1.1 %collective-permute-done.before.rest_0_ = f32[56,4,128]{2,1,0:T(4,128)S(1)} collective-permute-done((f32[56,4,128]{2,1,0:T(4,128)}, f32[56,4,128]{2,1,0:T(4,128)S(1)}, u32[]{:S(2)}, u32[]{:S(2)}) %collective-permute-start) | collective-permute-done | bytes 114720 | tf_op jit(solution)/shard_map/ppermute | solution.py:451
  10.9 5.1 %collective-permute-done.1.after.rest_1_ = f32[56,4,128]{2,1,0:T(4,128)S(1)} collective-permute-done((f32[56,4,128]{2,1,0:T(4,128)}, f32[56,4,128]{2,1,0:T(4,128)S(1)}, u32[]{:S(2)}, u32[]{:S(2)}) %collective-permute-start.1) | collective-permute-done | bytes 114720 | tf_op jit(solution)/shard_map/ppermute | solution.py:452
  16.2 1.9 %collective-permute-start.4 = (f32[11,4,512]{2,1,0:T(4,128)S(1)}, f32[11,4,512]{2,1,0:T(4,128)S(1)}, u32[]{:S(2)}, u32[]{:S(2)}) collective-permute-start(f32[11,4,512]{2,1,0:T(4,128)S(1)} %get-tuple-element.54), channel_id=1, source_target_pairs={{0,256},{256,512},{512,768},{1,257},{257,513},{513,769},{2,258},{2... | collective-permute-start | bytes 270344 | tf_op jit(solution)/shard_map/ppermute | solution.py:451
  18.2 5.1 %collective-permute-start.5 = (f32[11,4,512]{2,1,0:T(4,128)S(1)}, f32[11,4,512]{2,1,0:T(4,128)S(1)}, u32[]{:S(2)}, u32[]{:S(2)}) collective-permute-start(f32[11,4,512]{2,1,0:T(4,128)S(1)} %get-tuple-element.55), channel_id=1, source_target_pairs={{256,0},{512,256},{768,512},{257,1},{513,257},{769,513},{258,2},{5... | collective-permute-start | bytes 270344 | tf_op jit(solution)/shard_map/ppermute | solution.py:452
  23.3 5.0 %collective-permute-start.2 = (f32[8,4,512]{2,1,0:T(4,128)S(1)}, f32[8,4,512]{2,1,0:T(4,128)S(1)}, u32[]{:S(2)}, u32[]{:S(2)}) collective-permute-start(f32[8,4,512]{2,1,0:T(4,128)S(1)} %get-tuple-element.52), channel_id=1, source_target_pairs={{0,8},{8,16},{16,24},{24,32},{32,40},{40,48},{48,56},{56,64},{64,7... | collective-permute-start | bytes 196616 | tf_op jit(solution)/shard_map/ppermute | solution.py:451
  28.4 1.9 %collective-permute-start.3 = (f32[8,4,512]{2,1,0:T(4,128)S(1)}, f32[8,4,512]{2,1,0:T(4,128)S(1)}, u32[]{:S(2)}, u32[]{:S(2)}) collective-permute-start(f32[8,4,512]{2,1,0:T(4,128)S(1)} %get-tuple-element.53), channel_id=1, source_target_pairs={{8,0},{16,8},{24,16},{32,24},{40,32},{48,40},{56,48},{64,56},{72,6... | collective-permute-start | bytes 196616 | tf_op jit(solution)/shard_map/ppermute | solution.py:452
  30.3 5.4 %collective-permute-done.3.rest_1_ = f32[8,4,512]{2,1,0:T(4,128)S(1)} collective-permute-done((f32[8,4,512]{2,1,0:T(4,128)S(1)}, f32[8,4,512]{2,1,0:T(4,128)S(1)}, u32[]{:S(2)}, u32[]{:S(2)}) %collective-permute-start.3) | collective-permute-done | bytes 65568 | tf_op jit(solution)/shard_map/ppermute | solution.py:452
  35.8 0.9 copy-done.1
  36.7 0.9 copy-done.2
  37.7 1.2 %shard_map.158 = (f32[3,6,4,512]{3,2,1,0:T(4,128)S(1)}, f32[3,2,2,256]{3,2,1,0:T(2,128)S(1)}, f32[8,4,512]{2,1,0:T(4,128)S(1)}, f32[8,4,512]{2,1,0:T(4,128)S(1)}...) custom-call(f32[3,6,4,512]{3,2,1,0:T(4,128)S(1)} %get-tuple-element.44.fv, ...), custom_call_target="tpu_custom_call" | custom-call | flops 1000000 | bytes 1000000 | tf_op jit(solution)/shard_map/pallas_call | solution.py:434
  38.9 1.9 %collective-permute-start.8 = (f32[11,4,512]{2,1,0:T(4,128)S(1)}, f32[11,4,512]{2,1,0:T(4,128)S(1)}, u32[]{:S(2)}, u32[]{:S(2)}) collective-permute-start(f32[11,4,512]{2,1,0:T(4,128)S(1)} %get-tuple-element.61), channel_id=1, source_target_pairs={{0,256},{256,512},{512,768},{1,257},{257,513},{513,769},{2,258},{2... | collective-permute-start | bytes 270344 | tf_op jit(solution)/shard_map/ppermute | solution.py:451
  40.8 5.1 %collective-permute-start.9 = (f32[11,4,512]{2,1,0:T(4,128)S(1)}, f32[11,4,512]{2,1,0:T(4,128)S(1)}, u32[]{:S(2)}, u32[]{:S(2)}) collective-permute-start(f32[11,4,512]{2,1,0:T(4,128)S(1)} %get-tuple-element.62), channel_id=1, source_target_pairs={{256,0},{512,256},{768,512},{257,1},{513,257},{769,513},{258,2},{5... | collective-permute-start | bytes 270344 | tf_op jit(solution)/shard_map/ppermute | solution.py:452
  45.9 2.6 %collective-permute-start.6 = (f32[8,4,512]{2,1,0:T(4,128)S(1)}, f32[8,4,512]{2,1,0:T(4,128)S(1)}, u32[]{:S(2)}, u32[]{:S(2)}) collective-permute-start(f32[8,4,512]{2,1,0:T(4,128)S(1)} %get-tuple-element.59), channel_id=1, source_target_pairs={{0,8},{8,16},{16,24},{24,32},{32,40},{40,48},{48,56},{56,64},{64,7... | collective-permute-start | bytes 196616 | tf_op jit(solution)/shard_map/ppermute | solution.py:451
  48.6 3.2 %collective-permute-start.7 = (f32[8,4,512]{2,1,0:T(4,128)S(1)}, f32[8,4,512]{2,1,0:T(4,128)S(1)}, u32[]{:S(2)}, u32[]{:S(2)}) collective-permute-start(f32[8,4,512]{2,1,0:T(4,128)S(1)} %get-tuple-element.60), channel_id=1, source_target_pairs={{8,0},{16,8},{24,16},{32,24},{40,32},{48,40},{56,48},{64,56},{72,6... | collective-permute-start | bytes 196616 | tf_op jit(solution)/shard_map/ppermute | solution.py:452
  51.8 0.3 collective-permute-done.6.rest_6_
  52.1 3.8 %collective-permute-done.7.rest_7_ = f32[8,4,512]{2,1,0:T(4,128)S(1)} collective-permute-done((f32[8,4,512]{2,1,0:T(4,128)S(1)}, f32[8,4,512]{2,1,0:T(4,128)S(1)}, u32[]{:S(2)}, u32[]{:S(2)}) %collective-permute-start.7) | collective-permute-done | bytes 65568 | tf_op jit(solution)/shard_map/ppermute | solution.py:452
  56.0 3.3 %shard_map.159 = (f32[6,6,4,512]{3,2,1,0:T(4,128)S(1)}, f32[6,2,2,256]{3,2,1,0:T(2,128)S(1)}, f32[10,6,6,4,384]{4,3,2,1,0:T(4,128)S(1)}, f32[8,4,512]{2,1,0:T(4,...) custom-call(f32[3,6,4,512]{3,2,1,0:T(4,128)S(1)} %get-tuple-element.56.fv, ...), custom_call_target="tpu_custom_call" | custom-call | flops 10000000 | bytes 10000000 | tf_op jit(solution)/shard_map/pallas_call | solution.py:434
  59.3 1.9 %collective-permute-start.12 = (f32[11,4,512]{2,1,0:T(4,128)S(1)}, f32[11,4,512]{2,1,0:T(4,128)S(1)}, u32[]{:S(2)}, u32[]{:S(2)}) collective-permute-start(f32[11,4,512]{2,1,0:T(4,128)S(1)} %get-tuple-element.67), channel_id=1, source_target_pairs={{0,256},{256,512},{512,768},{1,257},{257,513},{513,769},{2,258},{2... | collective-permute-start | bytes 270344 | tf_op jit(solution)/shard_map/ppermute | solution.py:451
  61.2 5.1 %collective-permute-start.13 = (f32[11,4,512]{2,1,0:T(4,128)S(1)}, f32[11,4,512]{2,1,0:T(4,128)S(1)}, u32[]{:S(2)}, u32[]{:S(2)}) collective-permute-start(f32[11,4,512]{2,1,0:T(4,128)S(1)} %get-tuple-element.68), channel_id=1, source_target_pairs={{256,0},{512,256},{768,512},{257,1},{513,257},{769,513},{258,2},{5... | collective-permute-start | bytes 270344 | tf_op jit(solution)/shard_map/ppermute | solution.py:452
  66.4 3.6 %collective-permute-start.10 = (f32[8,4,512]{2,1,0:T(4,128)S(1)}, f32[8,4,512]{2,1,0:T(4,128)S(1)}, u32[]{:S(2)}, u32[]{:S(2)}) collective-permute-start(f32[8,4,512]{2,1,0:T(4,128)S(1)} %get-tuple-element.65), channel_id=1, source_target_pairs={{0,8},{8,16},{16,24},{24,32},{32,40},{40,48},{48,56},{56,64},{64,7... | collective-permute-start | bytes 196616 | tf_op jit(solution)/shard_map/ppermute | solution.py:451
  70.0 2.2 %collective-permute-start.11 = (f32[8,4,512]{2,1,0:T(4,128)S(1)}, f32[8,4,512]{2,1,0:T(4,128)S(1)}, u32[]{:S(2)}, u32[]{:S(2)}) collective-permute-start(f32[8,4,512]{2,1,0:T(4,128)S(1)} %get-tuple-element.66), channel_id=1, source_target_pairs={{8,0},{16,8},{24,16},{32,24},{40,32},{48,40},{56,48},{64,56},{72,6... | collective-permute-start | bytes 196616 | tf_op jit(solution)/shard_map/ppermute | solution.py:452
  72.5 4.8 %collective-permute-done.11.rest_1_ = f32[8,4,512]{2,1,0:T(4,128)S(1)} collective-permute-done((f32[8,4,512]{2,1,0:T(4,128)S(1)}, f32[8,4,512]{2,1,0:T(4,128)S(1)}, u32[]{:S(2)}, u32[]{:S(2)}) %collective-permute-start.11) | collective-permute-done | bytes 65568 | tf_op jit(solution)/shard_map/ppermute | solution.py:452
  77.4 1.2 %shard_map.160 = (f32[3,6,4,512]{3,2,1,0:T(4,128)S(1)}, f32[3,2,2,256]{3,2,1,0:T(2,128)S(1)}, f32[8,4,512]{2,1,0:T(4,128)S(1)}, f32[8,4,512]{2,1,0:T(4,128)S(1)}...) custom-call(f32[3,6,4,512]{3,2,1,0:T(4,128)S(1)} %get-tuple-element.56.fv, ...), custom_call_target="tpu_custom_call" | custom-call | flops 1000000 | bytes 1000000 | tf_op jit(solution)/shard_map/pallas_call | solution.py:434
  78.6 1.9 %collective-permute-start.16 = (f32[11,4,512]{2,1,0:T(4,128)S(1)}, f32[11,4,512]{2,1,0:T(4,128)S(1)}, u32[]{:S(2)}, u32[]{:S(2)}) collective-permute-start(f32[11,4,512]{2,1,0:T(4,128)S(1)} %get-tuple-element.74), channel_id=1, source_target_pairs={{0,256},{256,512},{512,768},{1,257},{257,513},{513,769},{2,258},{2... | collective-permute-start | bytes 270344 | tf_op jit(solution)/shard_map/ppermute | solution.py:451
  80.5 5.1 %collective-permute-start.17 = (f32[11,4,512]{2,1,0:T(4,128)S(1)}, f32[11,4,512]{2,1,0:T(4,128)S(1)}, u32[]{:S(2)}, u32[]{:S(2)}) collective-permute-start(f32[11,4,512]{2,1,0:T(4,128)S(1)} %get-tuple-element.75), channel_id=1, source_target_pairs={{256,0},{512,256},{768,512},{257,1},{513,257},{769,513},{258,2},{5... | collective-permute-start | bytes 270344 | tf_op jit(solution)/shard_map/ppermute | solution.py:452
  85.7 3.9 %collective-permute-start.14 = (f32[8,4,512]{2,1,0:T(4,128)S(1)}, f32[8,4,512]{2,1,0:T(4,128)S(1)}, u32[]{:S(2)}, u32[]{:S(2)}) collective-permute-start(f32[8,4,512]{2,1,0:T(4,128)S(1)} %get-tuple-element.72), channel_id=1, source_target_pairs={{0,8},{8,16},{16,24},{24,32},{32,40},{40,48},{48,56},{56,64},{64,7... | collective-permute-start | bytes 196616 | tf_op jit(solution)/shard_map/ppermute | solution.py:451
  89.6 1.9 %collective-permute-start.15 = (f32[8,4,512]{2,1,0:T(4,128)S(1)}, f32[8,4,512]{2,1,0:T(4,128)S(1)}, u32[]{:S(2)}, u32[]{:S(2)}) collective-permute-start(f32[8,4,512]{2,1,0:T(4,128)S(1)} %get-tuple-element.73), channel_id=1, source_target_pairs={{8,0},{16,8},{24,16},{32,24},{40,32},{48,40},{56,48},{64,56},{72,6... | collective-permute-start | bytes 196616 | tf_op jit(solution)/shard_map/ppermute | solution.py:452
  91.9 5.1 %collective-permute-done.15.rest_5_ = f32[8,4,512]{2,1,0:T(4,128)S(1)} collective-permute-done((f32[8,4,512]{2,1,0:T(4,128)S(1)}, f32[8,4,512]{2,1,0:T(4,128)S(1)}, u32[]{:S(2)}, u32[]{:S(2)}) %collective-permute-start.15) | collective-permute-done | bytes 65568 | tf_op jit(solution)/shard_map/ppermute | solution.py:452
  97.0 3.2 %shard_map.161 = (f32[6,6,4,384]{3,2,1,0:T(4,128)}, f32[6,2,2,128]{3,2,1,0:T(2,128)}, f32[3,6,4,384]{3,2,1,0:T(4,128)}, f32[3,2,2,128]{3,2,1,0:T(2,128)}) custom-call(f32[3,6,4,512]{3,2,1,0:T(4,128)S(1)} %get-tuple-element.69.fv, f32[3,2,2,256]{3,2,1,0:T(2,128)S(1)} %get-tuple-element.70.cv, f32[6,6,4,512]{3,2,1,0:T(4,128)S(1)} %get-tuple-element.63.fs, ...), custom_call_target="tpu_custom_call" | custom-call | flops 10000000 | bytes 10000000 | tf_op jit(solution)/shard_map/pallas_call | solution.py:434
  (40 shorter events, 0.8 us)
Async XLA Ops:
  0.6 15.4 %copy-start.9 = (s32[2,2,128]{2,1,0:T(2,128)S(1)}, s32[2,2,128]{2,1,0:T(2,128)}, u32[]{:S(2)}) copy-start(s32[2,2,128]{2,1,0:T(2,128)} %czone.1) | copy-start | bytes 6148
  0.6 15.4 %copy-start.7 = (f32[6,2,2,128]{3,2,1,0:T(2,128)S(1)}, f32[6,2,2,128]{3,2,1,0:T(2,128)}, u32[]{:S(2)}) copy-start(f32[6,2,2,128]{3,2,1,0:T(2,128)} %cs.1) | copy-start | bytes 36868
  0.7 15.4 %copy-start.8 = (f32[3,2,2,128]{3,2,1,0:T(2,128)S(1)}, f32[3,2,2,128]{3,2,1,0:T(2,128)}, u32[]{:S(2)}) copy-start(f32[3,2,2,128]{3,2,1,0:T(2,128)} %cv.1) | copy-start | bytes 18436
  0.7 15.4 %copy-start.6 = (s32[4,6,384]{2,0,1:T(4,128)S(1)}, s32[4,6,384]{2,0,1:T(4,128)}, u32[]{:S(2)}) copy-start(s32[4,6,384]{2,0,1:T(4,128)} %param.20) | copy-start | bytes 110596
  0.7 15.4 %copy-start.5 = (s32[4,6,384]{2,0,1:T(4,128)S(1)}, s32[4,6,384]{2,0,1:T(4,128)}, u32[]{:S(2)}) copy-start(s32[4,6,384]{2,0,1:T(4,128)} %param.18) | copy-start | bytes 110596
  0.7 15.4 %copy-start.3 = (f32[6,4,6,384]{3,1,2,0:T(4,128)S(1)}, f32[6,4,6,384]{3,1,2,0:T(4,128)}, u32[]{:S(2)}) copy-start(f32[6,4,6,384]{3,1,2,0:T(4,128)} %param.14) | copy-start | bytes 663556
  0.7 15.4 %copy-start.4 = (f32[3,4,6,384]{3,1,2,0:T(4,128)S(1)}, f32[3,4,6,384]{3,1,2,0:T(4,128)}, u32[]{:S(2)}) copy-start(f32[3,4,6,384]{3,1,2,0:T(4,128)} %param.13) | copy-start | bytes 331780
  0.7 35.0 %copy-start.10 = (f32[16]{0:T(128)S(1)}, f32[16]{0:T(128)}, u32[]{:S(2)}) copy-start(f32[16]{0:T(128)} %table.3) | copy-start | bytes 196
  0.7 55.2 %copy-start = (f32[10,6,4,6,384]{4,2,3,1,0:T(4,128)S(1)}, f32[10,6,4,6,384]{4,2,3,1,0:T(4,128)}, u32[]{:S(2)}) copy-start(f32[10,6,4,6,384]{4,2,3,1,0:T(4,128)} %param.17) | copy-start | bytes 6635524
  0.7 55.2 %copy-start.11 = (f32[16]{0:T(128)S(1)}, f32[16]{0:T(128)}, u32[]{:S(2)}) copy-start(f32[16]{0:T(128)} %rest_0_.1) | copy-start | bytes 196
  0.7 55.2 %copy-start.12 = (f32[16]{0:T(128)S(1)}, f32[16]{0:T(128)}, u32[]{:S(2)}) copy-start(f32[16]{0:T(128)} %rest_1_.1) | copy-start | bytes 196
  0.7 55.2 %copy-start.13 = (f32[10]{0:T(128)S(1)}, f32[10]{0:T(128)}, u32[]{:S(2)}) copy-start(f32[10]{0:T(128)} %rest_2_.3) | copy-start | bytes 124
  0.8 55.2 %copy-start.14 = (f32[10]{0:T(128)S(1)}, f32[10]{0:T(128)}, u32[]{:S(2)}) copy-start(f32[10]{0:T(128)} %rest_3_.3) | copy-start | bytes 124
  3.9 7.0 %collective-permute-start = (f32[56,4,128]{2,1,0:T(4,128)}, f32[56,4,128]{2,1,0:T(4,128)S(1)}, u32[]{:S(2)}, u32[]{:S(2)}) collective-permute-start(f32[56,4,128]{2,1,0:T(4,128)} %get-tuple-element.42), channel_id=1, source_target_pairs={{0,1},{1,2},{2,3},{3,4},{4,5},{5,6},{6,7},{8,9},{9,10},{10,11},{11... | collective-permute-start | bytes 344072 | tf_op jit(solution)/shard_map/ppermute | solution.py:451
  7.0 9.0 %collective-permute-start.1 = (f32[56,4,128]{2,1,0:T(4,128)}, f32[56,4,128]{2,1,0:T(4,128)S(1)}, u32[]{:S(2)}, u32[]{:S(2)}) collective-permute-start(f32[56,4,128]{2,1,0:T(4,128)} %get-tuple-element.43), channel_id=1, source_target_pairs={{1,0},{2,1},{3,2},{4,3},{5,4},{6,5},{7,6},{9,8},{10,9},{11,10},{12... | collective-permute-start | bytes 344072 | tf_op jit(solution)/shard_map/ppermute | solution.py:452
  16.2 19.5 %collective-permute-start.4 = (f32[11,4,512]{2,1,0:T(4,128)S(1)}, f32[11,4,512]{2,1,0:T(4,128)S(1)}, u32[]{:S(2)}, u32[]{:S(2)}) collective-permute-start(f32[11,4,512]{2,1,0:T(4,128)S(1)} %get-tuple-element.54), channel_id=1, source_target_pairs={{0,256},{256,512},{512,768},{1,257},{257,513},{513,769},{2,258},{2... | collective-permute-start | bytes 270344 | tf_op jit(solution)/shard_map/ppermute | solution.py:451
  18.2 17.6 %collective-permute-start.5 = (f32[11,4,512]{2,1,0:T(4,128)S(1)}, f32[11,4,512]{2,1,0:T(4,128)S(1)}, u32[]{:S(2)}, u32[]{:S(2)}) collective-permute-start(f32[11,4,512]{2,1,0:T(4,128)S(1)} %get-tuple-element.55), channel_id=1, source_target_pairs={{256,0},{512,256},{768,512},{257,1},{513,257},{769,513},{258,2},{5... | collective-permute-start | bytes 270344 | tf_op jit(solution)/shard_map/ppermute | solution.py:452
  23.3 7.0 %collective-permute-start.2 = (f32[8,4,512]{2,1,0:T(4,128)S(1)}, f32[8,4,512]{2,1,0:T(4,128)S(1)}, u32[]{:S(2)}, u32[]{:S(2)}) collective-permute-start(f32[8,4,512]{2,1,0:T(4,128)S(1)} %get-tuple-element.52), channel_id=1, source_target_pairs={{0,8},{8,16},{16,24},{24,32},{32,40},{40,48},{48,56},{56,64},{64,7... | collective-permute-start | bytes 196616 | tf_op jit(solution)/shard_map/ppermute | solution.py:451
  28.4 7.4 %collective-permute-start.3 = (f32[8,4,512]{2,1,0:T(4,128)S(1)}, f32[8,4,512]{2,1,0:T(4,128)S(1)}, u32[]{:S(2)}, u32[]{:S(2)}) collective-permute-start(f32[8,4,512]{2,1,0:T(4,128)S(1)} %get-tuple-element.53), channel_id=1, source_target_pairs={{8,0},{16,8},{24,16},{32,24},{40,32},{48,40},{56,48},{64,56},{72,6... | collective-permute-start | bytes 196616 | tf_op jit(solution)/shard_map/ppermute | solution.py:452
  35.7 1.0 copy-start.1
  38.9 17.1 %collective-permute-start.8 = (f32[11,4,512]{2,1,0:T(4,128)S(1)}, f32[11,4,512]{2,1,0:T(4,128)S(1)}, u32[]{:S(2)}, u32[]{:S(2)}) collective-permute-start(f32[11,4,512]{2,1,0:T(4,128)S(1)} %get-tuple-element.61), channel_id=1, source_target_pairs={{0,256},{256,512},{512,768},{1,257},{257,513},{513,769},{2,258},{2... | collective-permute-start | bytes 270344 | tf_op jit(solution)/shard_map/ppermute | solution.py:451
  40.8 15.2 %collective-permute-start.9 = (f32[11,4,512]{2,1,0:T(4,128)S(1)}, f32[11,4,512]{2,1,0:T(4,128)S(1)}, u32[]{:S(2)}, u32[]{:S(2)}) collective-permute-start(f32[11,4,512]{2,1,0:T(4,128)S(1)} %get-tuple-element.62), channel_id=1, source_target_pairs={{256,0},{512,256},{768,512},{257,1},{513,257},{769,513},{258,2},{5... | collective-permute-start | bytes 270344 | tf_op jit(solution)/shard_map/ppermute | solution.py:452
  45.9 6.2 %collective-permute-start.6 = (f32[8,4,512]{2,1,0:T(4,128)S(1)}, f32[8,4,512]{2,1,0:T(4,128)S(1)}, u32[]{:S(2)}, u32[]{:S(2)}) collective-permute-start(f32[8,4,512]{2,1,0:T(4,128)S(1)} %get-tuple-element.59), channel_id=1, source_target_pairs={{0,8},{8,16},{16,24},{24,32},{32,40},{40,48},{48,56},{56,64},{64,7... | collective-permute-start | bytes 196616 | tf_op jit(solution)/shard_map/ppermute | solution.py:451
  48.6 7.4 %collective-permute-start.7 = (f32[8,4,512]{2,1,0:T(4,128)S(1)}, f32[8,4,512]{2,1,0:T(4,128)S(1)}, u32[]{:S(2)}, u32[]{:S(2)}) collective-permute-start(f32[8,4,512]{2,1,0:T(4,128)S(1)} %get-tuple-element.60), channel_id=1, source_target_pairs={{8,0},{16,8},{24,16},{32,24},{40,32},{48,40},{56,48},{64,56},{72,6... | collective-permute-start | bytes 196616 | tf_op jit(solution)/shard_map/ppermute | solution.py:452
  59.3 18.1 %collective-permute-start.12 = (f32[11,4,512]{2,1,0:T(4,128)S(1)}, f32[11,4,512]{2,1,0:T(4,128)S(1)}, u32[]{:S(2)}, u32[]{:S(2)}) collective-permute-start(f32[11,4,512]{2,1,0:T(4,128)S(1)} %get-tuple-element.67), channel_id=1, source_target_pairs={{0,256},{256,512},{512,768},{1,257},{257,513},{513,769},{2,258},{2... | collective-permute-start | bytes 270344 | tf_op jit(solution)/shard_map/ppermute | solution.py:451
  61.2 16.2 %collective-permute-start.13 = (f32[11,4,512]{2,1,0:T(4,128)S(1)}, f32[11,4,512]{2,1,0:T(4,128)S(1)}, u32[]{:S(2)}, u32[]{:S(2)}) collective-permute-start(f32[11,4,512]{2,1,0:T(4,128)S(1)} %get-tuple-element.68), channel_id=1, source_target_pairs={{256,0},{512,256},{768,512},{257,1},{513,257},{769,513},{258,2},{5... | collective-permute-start | bytes 270344 | tf_op jit(solution)/shard_map/ppermute | solution.py:452
  66.4 6.2 %collective-permute-start.10 = (f32[8,4,512]{2,1,0:T(4,128)S(1)}, f32[8,4,512]{2,1,0:T(4,128)S(1)}, u32[]{:S(2)}, u32[]{:S(2)}) collective-permute-start(f32[8,4,512]{2,1,0:T(4,128)S(1)} %get-tuple-element.65), channel_id=1, source_target_pairs={{0,8},{8,16},{16,24},{24,32},{32,40},{40,48},{48,56},{56,64},{64,7... | collective-permute-start | bytes 196616 | tf_op jit(solution)/shard_map/ppermute | solution.py:451
  70.0 7.4 %collective-permute-start.11 = (f32[8,4,512]{2,1,0:T(4,128)S(1)}, f32[8,4,512]{2,1,0:T(4,128)S(1)}, u32[]{:S(2)}, u32[]{:S(2)}) collective-permute-start(f32[8,4,512]{2,1,0:T(4,128)S(1)} %get-tuple-element.66), channel_id=1, source_target_pairs={{8,0},{16,8},{24,16},{32,24},{40,32},{48,40},{56,48},{64,56},{72,6... | collective-permute-start | bytes 196616 | tf_op jit(solution)/shard_map/ppermute | solution.py:452
  78.6 18.4 %collective-permute-start.16 = (f32[11,4,512]{2,1,0:T(4,128)S(1)}, f32[11,4,512]{2,1,0:T(4,128)S(1)}, u32[]{:S(2)}, u32[]{:S(2)}) collective-permute-start(f32[11,4,512]{2,1,0:T(4,128)S(1)} %get-tuple-element.74), channel_id=1, source_target_pairs={{0,256},{256,512},{512,768},{1,257},{257,513},{513,769},{2,258},{2... | collective-permute-start | bytes 270344 | tf_op jit(solution)/shard_map/ppermute | solution.py:451
  80.5 16.5 %collective-permute-start.17 = (f32[11,4,512]{2,1,0:T(4,128)S(1)}, f32[11,4,512]{2,1,0:T(4,128)S(1)}, u32[]{:S(2)}, u32[]{:S(2)}) collective-permute-start(f32[11,4,512]{2,1,0:T(4,128)S(1)} %get-tuple-element.75), channel_id=1, source_target_pairs={{256,0},{512,256},{768,512},{257,1},{513,257},{769,513},{258,2},{5... | collective-permute-start | bytes 270344 | tf_op jit(solution)/shard_map/ppermute | solution.py:452
  85.7 6.2 %collective-permute-start.14 = (f32[8,4,512]{2,1,0:T(4,128)S(1)}, f32[8,4,512]{2,1,0:T(4,128)S(1)}, u32[]{:S(2)}, u32[]{:S(2)}) collective-permute-start(f32[8,4,512]{2,1,0:T(4,128)S(1)} %get-tuple-element.72), channel_id=1, source_target_pairs={{0,8},{8,16},{16,24},{24,32},{32,40},{40,48},{48,56},{56,64},{64,7... | collective-permute-start | bytes 196616 | tf_op jit(solution)/shard_map/ppermute | solution.py:451
  89.6 7.4 %collective-permute-start.15 = (f32[8,4,512]{2,1,0:T(4,128)S(1)}, f32[8,4,512]{2,1,0:T(4,128)S(1)}, u32[]{:S(2)}, u32[]{:S(2)}) collective-permute-start(f32[8,4,512]{2,1,0:T(4,128)S(1)} %get-tuple-element.73), channel_id=1, source_target_pairs={{8,0},{16,8},{24,16},{32,24},{40,32},{48,40},{56,48},{64,56},{72,6... | collective-permute-start | bytes 196616 | tf_op jit(solution)/shard_map/ppermute | solution.py:452
  (1 other events, 0.9 us)
